TPU v7x, 512 devices: a whole 4x8x8 slice. The times are simulated.
512 devices in a mesh: tm: 8 (over z), gx: 8 (over x, core), gy: 8 (over y).
Axes of the slice: x: 4, y: 8, z: 8, core: 2. Of those that a mesh axis runs over, the one named last changes fastest.
Arguments:
- initial: float32 [64, 64, 1024], P(None, 'gx', 'gy'), may hold values from -6 to 6
- capacity: float32 [64, 64, 1024], P(None, 'gx', 'gy'), may hold values from 0.25 to 4
- profile: float32 [64], replicated, may hold values from 0.5 to 1.5
- bore_loop: int32 [64, 1024], P('gx', 'gy'), may hold values from 0 to 31, as said below
- plan: int32 [8, 2, 16], P('tm'), may hold values from 0 to 7
Outputs:
- states: float32 [8, 64, 64, 1024], P('tm', None, 'gx', 'gy')
Inputs may be any that keep to these rules, and one draw needn't show every extreme that they name: `bore_loop`: a column holds a borehole of circuit v when v < 16; values of 16 or more mark columns without a borehole; all boreholes lie in one lateral rectangle of 16 to 32 rows and 256 to 512 columns, placed anywhere.
All inputs are finite; a program needn't handle non-finite values.
Results may differ from a plain program's by a relative error of at most 0.0001.
Values sent between devices are 32-bit elements; how exact they have to be, the bound alone decides.
A program may use at most 64 MiB of HBM per device.

v0:
```python
from functools import partial

import jax
import jax.numpy as jnp
import numpy as np
from jax import lax
from jax.sharding import PartitionSpec as P

STEPS = 2
ITERS = 3
TERMS = 8
LOOPS = 16


HORIZON = 4.0 / 3.0
EXPONENT = 16.0


def with_halo(cells, sides, width):
    for axis, dim in sides:
        count = lax.axis_size(axis)
        ends = count - 1
        head = lax.slice_in_dim(cells, 0, width, axis=dim)
        tail = lax.slice_in_dim(cells, cells.shape[dim] - width, cells.shape[dim], axis=dim)
        cells = jnp.concatenate(
            [
                lax.ppermute(tail, axis, [(i, (i + 1) % count) for i in range(ends)]),
                cells,
                lax.ppermute(head, axis, [((i + 1) % count, i) for i in range(ends)]),
            ],
            axis=dim,
        )
    return cells


def from_behind(value, axis, steps):
    count = lax.axis_size(axis)
    first, last = (max(0, -steps), min(count, count - steps))
    return lax.ppermute(value, axis, [(source, source + steps) for source in range(first, last)])


def cheb_coeffs(term_count):
    angles = np.pi * (np.arange(term_count) + 0.5) / term_count
    cheb_nodes = np.cos(angles)
    samples = np.exp(-EXPONENT * (cheb_nodes + 1.0))
    coeffs = [
        2.0 / term_count * float(np.sum(samples * np.cos(term_index * angles)))
        for term_index in range(term_count)
    ]
    coeffs[0] = coeffs[0] / 2.0
    return coeffs


def stencil(padded):
    beside_all = padded[2:, 1:-1, 1:-1] + padded[:-2, 1:-1, 1:-1]
    beside_all = beside_all + padded[1:-1, 2:, 1:-1] + padded[1:-1, :-2, 1:-1]
    beside_all = beside_all + padded[1:-1, 1:-1, 2:] + padded[1:-1, 1:-1, :-2]
    return 6.0 * padded[1:-1, 1:-1, 1:-1] - beside_all


def cg_stiffness(vector):
    wide_state = with_halo(vector, (("gx", 1), ("gy", 2)), 1)
    return stencil(jnp.pad(wide_state, ((1, 1), (0, 0), (0, 0))))


def poly_stiffness(vector):
    wide_state = with_halo(vector, (("gx", 1), ("gy", 2)), 1)
    return stencil(jnp.pad(wide_state, ((1, 1), (0, 0), (0, 0))))


def chebyshev(start_vec, apply_shifted, coeffs):
    previous = start_vec
    current = apply_shifted(start_vec)
    accumulated = coeffs[0] * previous + coeffs[1] * current
    for term_index in range(2, len(coeffs)):
        following = 2.0 * apply_shifted(current) - previous
        accumulated = accumulated + coeffs[term_index] * following
        previous, current = (current, following)
    return accumulated


def shifted_local(vector, inverse_cap, span_scale):
    return span_scale * poly_stiffness(vector) * inverse_cap - vector


def residual_inner(residual, precond):
    return lax.psum(jnp.sum(residual * precond), ("gx", "gy"))


def solve_slice(start_vec, capacity, profile, bore_loop, slice_table, slice_length):
    time_step = slice_length / STEPS
    mass_term = capacity / time_step
    diagonal = mass_term + 6.0
    loop_ids = jnp.arange(LOOPS, dtype=jnp.int32)
    matches = bore_loop[None, :, :] == loop_ids[:, None, None]
    current_state = start_vec
    for step_index in range(STEPS):
        rate_table = slice_table[step_index].astype(jnp.float32) - 3.5
        column = jnp.sum(jnp.where(matches, rate_table[:, None, None], jnp.float32(0.0)), axis=0)
        right_side = mass_term * current_state + profile[:, None, None] * column[None, :, :]
        solution = current_state
        residual = right_side - (mass_term * solution + cg_stiffness(solution))
        precond = residual / diagonal
        inner_now = residual_inner(residual, precond)
        direction = precond
        for iteration in range(ITERS):
            applied = mass_term * direction + cg_stiffness(direction)
            curvature = lax.psum(jnp.sum(direction * applied), ("gx", "gy"))
            step_size = inner_now / curvature
            solution = solution + step_size * direction
            residual = residual - step_size * applied
            if iteration + 1 < ITERS:
                precond = residual / diagonal
                inner_next = residual_inner(residual, precond)
                direction = precond + inner_next / inner_now * direction
                inner_now = inner_next
        current_state = solution
    return current_state


def per_device(initial, capacity, profile, bore_loop, plan):
    slice_total = lax.axis_size("tm")
    slice_length = HORIZON / slice_total
    is_first = (lax.axis_index("tm") == 0).astype(jnp.float32)
    slice_end = solve_slice(initial * is_first, capacity, profile, bore_loop, plan[0], slice_length)
    section_count = slice_total.bit_length() - 1
    coeffs = cheb_coeffs(TERMS)
    inverse_cap = 1.0 / capacity
    states = slice_end
    for section_index in range(section_count):
        earlier = from_behind(states, "tm", 1 << section_index)
        span_scale = (1 << section_index) / (12.0 * slice_total)
        apply_shifted = partial(shifted_local, inverse_cap=inverse_cap, span_scale=span_scale)
        states = states + chebyshev(earlier, apply_shifted, coeffs)
    return states[None]


def solution(mesh):
    return jax.shard_map(
        per_device,
        mesh=mesh,
        in_specs=(
            P(None, "gx", "gy"),
            P(None, "gx", "gy"),
            P(),
            P("gx", "gy"),
            P("tm", None, None),
        ),
        out_specs=P("tm", None, "gx", "gy"),
        check_vma=False,
    )
```

profile of v0, /device:TPU:161, one launch (start us, length us, event | category | flops | bytes accessed | tf_op | source)
XLA Modules:
  0.0 2073.6 jit_solution(16718925928475843402)
XLA Ops:
  58.1 104.0 %all-reduce.30 = (f32[]{:T(128)}, f32[]{:T(128)}) all-reduce(f32[]{:T(128)} %get-tuple-element.8, f32[]{:T(128)} %get-tuple-element.7), channel_id=1, replica_groups=mesh['tm'=8,'gx'=8,'gy'=8] {'gx','gy'}, use_global_device_ids=true, to_apply=%region_2.3 | all-reduce | flops 2 | bytes 16 | tf_op jit(solution)/shard_map/psum | solution.py:87
  164.1 125.6 %psum.86 = f32[]{:T(128)} all-reduce(f32[]{:T(128)} %get-tuple-element.24), channel_id=1, replica_groups=mesh['tm'=8,'gx'=8,'gy'=8] {'gx','gy'}, use_global_device_ids=true, to_apply=%region_6.7 | all-reduce | flops 1 | bytes 8 | tf_op jit(solution)/shard_map/psum | solution.py:87
  293.1 13.5 collective-permute-start.9
  331.1 110.9 %psum.87 = f32[]{:T(128)} all-reduce(f32[]{:T(128)} %get-tuple-element.22), channel_id=1, replica_groups=mesh['tm'=8,'gx'=8,'gy'=8] {'gx','gy'}, use_global_device_ids=true, to_apply=%region_8.9 | all-reduce | flops 1 | bytes 8 | tf_op jit(solution)/shard_map/psum | solution.py:108
  444.0 124.9 %psum.88 = f32[]{:T(128)} all-reduce(f32[]{:T(128)} %multiply_reduce_fusion.5), channel_id=1, replica_groups=mesh['tm'=8,'gx'=8,'gy'=8] {'gx','gy'}, use_global_device_ids=true, to_apply=%region_10.11 | all-reduce | flops 1 | bytes 8 | tf_op jit(solution)/shard_map/psum | solution.py:87
  572.2 13.2 collective-permute-start.13
  610.9 110.6 %psum.89 = f32[]{:T(128)} all-reduce(f32[]{:T(128)} %fusion.246), channel_id=1, replica_groups=mesh['tm'=8,'gx'=8,'gy'=8] {'gx','gy'}, use_global_device_ids=true, to_apply=%region_12.13 | all-reduce | flops 1 | bytes 8 | tf_op jit(solution)/shard_map/psum | solution.py:108
  724.9 13.5 collective-permute-start.17
  773.9 9.4 collective-permute-done.23
  789.9 108.2 %all-reduce.29 = (f32[]{:T(128)}, f32[]{:T(128)}) all-reduce(f32[]{:T(128)} %get-tuple-element.6, f32[]{:T(128)} %get-tuple-element.5), channel_id=1, replica_groups=mesh['tm'=8,'gx'=8,'gy'=8] {'gx','gy'}, use_global_device_ids=true, to_apply=%region_15.16 | all-reduce | flops 2 | bytes 16 | tf_op jit(solution)/shard_map/psum | solution.py:87
  900.1 125.0 %psum.92 = f32[]{:T(128)} all-reduce(f32[]{:T(128)} %get-tuple-element.17), channel_id=1, replica_groups=mesh['tm'=8,'gx'=8,'gy'=8] {'gx','gy'}, use_global_device_ids=true, to_apply=%region_19.20 | all-reduce | flops 1 | bytes 8 | tf_op jit(solution)/shard_map/psum | solution.py:87
  1028.4 13.2 collective-permute-start.25
  1067.1 110.5 %psum.93 = f32[]{:T(128)} all-reduce(f32[]{:T(128)} %get-tuple-element.15), channel_id=1, replica_groups=mesh['tm'=8,'gx'=8,'gy'=8] {'gx','gy'}, use_global_device_ids=true, to_apply=%region_21.22 | all-reduce | flops 1 | bytes 8 | tf_op jit(solution)/shard_map/psum | solution.py:108
  1179.6 124.8 %psum.94 = f32[]{:T(128)} all-reduce(f32[]{:T(128)} %multiply_reduce_fusion), channel_id=1, replica_groups=mesh['tm'=8,'gx'=8,'gy'=8] {'gx','gy'}, use_global_device_ids=true, to_apply=%region_23.24 | all-reduce | flops 1 | bytes 8 | tf_op jit(solution)/shard_map/psum | solution.py:87
  1307.8 13.2 collective-permute-start.29
  1346.4 110.6 %psum.95 = f32[]{:T(128)} all-reduce(f32[]{:T(128)} %fusion.219), channel_id=1, replica_groups=mesh['tm'=8,'gx'=8,'gy'=8] {'gx','gy'}, use_global_device_ids=true, to_apply=%region_25.26 | all-reduce | flops 1 | bytes 8 | tf_op jit(solution)/shard_map/psum | solution.py:108
  1467.7 14.4 collective-permute-start.34
  1517.5 9.6 collective-permute-done.40
  1573.0 9.4 collective-permute-done.48
  1599.8 9.4 collective-permute-done.52
  1626.2 9.4 collective-permute-done.56
  1652.5 9.4 collective-permute-done.60
  1674.4 11.7 collective-permute-done.61
  1698.8 9.4 collective-permute-done.65
  1777.9 9.4 collective-permute-done.77
  1804.3 9.4 collective-permute-done.81
  1857.0 9.4 collective-permute-done.89
  1876.2 11.7 collective-permute-done.90
  1927.1 9.4 collective-permute-done.98
  1953.5 9.4 collective-permute-done.102
  1979.8 9.4 collective-permute-done.106
  2032.6 9.4 collective-permute-done.114
  (382 shorter events, 667.2 us)
Async XLA Ops:
  307.7 16.4 collective-permute-start.11
  313.2 15.9 collective-permute-start.10
  586.6 17.3 collective-permute-start.15
  593.0 15.9 collective-permute-start.14
  743.5 15.9 collective-permute-start.18
  772.0 15.9 collective-permute-start.22
  1042.8 17.3 collective-permute-start.27
  1049.2 15.9 collective-permute-start.26
  1322.2 17.3 collective-permute-start.31
  1328.6 15.9 collective-permute-start.30
  1465.8 16.4 collective-permute-start.33
  1487.3 15.9 collective-permute-start.35
  1515.6 15.9 collective-permute-start.39
  1542.9 15.9 collective-permute-start.43
  1569.8 15.9 collective-permute-start.47
  1596.5 15.6 collective-permute-start.51
  1622.8 15.6 collective-permute-start.55
  1649.2 15.6 collective-permute-start.59
  1666.1 19.9 collective-permute-start.61
  1695.5 15.6 collective-permute-start.64
  1721.8 15.6 collective-permute-start.68
  1748.2 15.6 collective-permute-start.72
  1774.6 15.6 collective-permute-start.76
  1800.9 15.6 collective-permute-start.80
  1827.3 15.6 collective-permute-start.84
  1853.6 15.6 collective-permute-start.88
  1870.6 17.3 collective-permute-start.90
  1897.4 15.6 collective-permute-start.93
  1923.7 15.6 collective-permute-start.97
  1950.1 15.6 collective-permute-start.101
  1976.5 15.6 collective-permute-start.105
  2002.8 15.6 collective-permute-start.109
  (91 other events, 967.8 us)
where the time goes:
time: 2090 us; the launch traced here: 2070 us
  blocking collectives  1150 us (55%)
  waiting for transfers between devices  464 us (22%)
  starting transfers between devices  381 us (18%)
  other arithmetic  51.2 us (2%)
    psum x6, blocking collectives, residual_inner(): return lax.psum(jnp.sum(residual * precond), ('gx', 'gy'))  712 us
    psum x4, blocking collectives, solve_slice(): curvature = lax.psum(jnp.sum(direction * applied), ('gx', 'gy'))  443 us
    ppermute x58, waiting for transfers between devices, with_halo(): lax.ppermute(head, axis, [((i + 1) % count, i) for i in range(ends)])  337 us
    ppermute x58, starting transfers between devices, with_halo(): lax.ppermute(head, axis, [((i + 1) % count, i) for i in range(ends)])  217 us
    ppermute x58, starting transfers between devices, with_halo(): lax.ppermute(tail, axis, [(i, (i + 1) % count) for i in range(ends)])  146 us
    ppermute x58, waiting for transfers between devices, with_halo(): lax.ppermute(tail, axis, [(i, (i + 1) % count) for i in range(ends)])  100 us
  transfers between devices with their start and end apart: 119, of which 90 were waited for; matrix products, arithmetic and copies ran while one was open for 0% of the time, Pallas kernels for 0%

commit v1 on v0

v1 whole, which is shorter than its diff:
```python
import functools

import jax
import jax.numpy as jnp
import numpy as np
from jax import lax
from jax.experimental import pallas as pl
from jax.experimental.pallas import tpu as pltpu
from jax.sharding import PartitionSpec as P

MESH = pl.DeviceIdType.MESH
STEPS = 2
TERMS = 8
LOOPS = 16
HORIZON = 4.0 / 3.0
EXPONENT = 16.0

NZ, NXL, NYL = 64, 8, 128
HALF = NXL // 2
REACH = TERMS - 1
OWN = REACH
WIDE = REACH + HALF
LAST = WIDE - 1
ROWS = NYL + 32
LOW, HIGH = 16, 16 + NYL
CHUNK = 8


def cheb_coeffs(term_count):
    angles = np.pi * (np.arange(term_count) + 0.5) / term_count
    cheb_nodes = np.cos(angles)
    samples = np.exp(-EXPONENT * (cheb_nodes + 1.0))
    coeffs = [
        2.0 / term_count * float(np.sum(samples * np.cos(term_index * angles)))
        for term_index in range(term_count)
    ]
    coeffs[0] = coeffs[0] / 2.0
    return coeffs


def chunks(low, high):
    return [(r, min(CHUNK, high - r)) for r in range(low, high, CHUNK)]


ALL_ROWS = (LOW - 8, HIGH + 8)
OWN_ROWS = (LOW, HIGH)


def kernel(
    sizes,
    init_hbm, cap_hbm, prof_ref, bore_ref, plan_ref, out_ref,
    nat, pool, src, xbuf, hbuf, bext, plans, rates, mom, pay, coef, sums_x, sums_y,
    load_sem, bore_send, bore_recv, plan_send, plan_recv, halo_send, halo_recv,
    sum_send, sum_recv, shift_send, shift_recv,
):
    slices, nx, ny = sizes
    slots = max(1, slices // 2)
    inv_step = STEPS * slices / HORIZON
    tm, gx, gy = lax.axis_index("tm"), lax.axis_index("gx"), lax.axis_index("gy")
    f32 = jnp.float32
    cheb = cheb_coeffs(TERMS)

    INV, DINV, U0, KU = 0, 1, 2, 3
    CA, CG = 4, 5
    X = 6
    V = X + slots
    TS = V
    ZX = V + max(3 * slots, TERMS - 1)

    def has(a, b):
        x, y = gx + a, gy + b
        return (x >= 0) & (x < nx) & (y >= 0) & (y < ny)

    around = [(a, b) for b in (-1, 0, 1) for a in (-1, 0, 1) if (a, b) != (0, 0)]
    around.sort(key=lambda ab: ab[1] == 0)
    pending = []

    load_cap = pltpu.make_async_copy(cap_hbm, nat.at[0], load_sem.at[0])
    load_init = pltpu.make_async_copy(init_hbm, nat.at[1], load_sem.at[1])
    load_cap.start()
    load_init.start()

    barrier = pltpu.get_barrier_semaphore()
    for d in range(1, nx):
        pl.semaphore_signal(barrier, inc=1, device_id={"gx": lax.rem(gx + d, nx)}, device_id_type=MESH)
    for d in range(1, ny):
        pl.semaphore_signal(barrier, inc=1, device_id={"gy": lax.rem(gy + d, ny)}, device_id_type=MESH)
    for a, b in around:
        if a and b:
            @pl.when(has(a, b))
            def _():
                pl.semaphore_signal(barrier, inc=1, device_id={"gx": gx + a, "gy": gy + b}, device_id_type=MESH)
    spans = [1] + [2 * s for s in range(1, slots)]
    for s in spans:
        @pl.when(tm >= s)
        def _():
            pl.semaphore_signal(barrier, inc=1, device_id={"tm": tm - s}, device_id_type=MESH)
    greeted = nx - 1 + ny - 1
    for a, b in around:
        if a and b:
            greeted = greeted + jnp.where(has(a, b), 1, 0)
    for s in spans:
        greeted = greeted + jnp.where(tm + s < slices, 1, 0)
    pl.semaphore_wait(barrier, greeted)

    lane = lax.broadcasted_iota(jnp.int32, (8, 128), 1)
    lane_c = lax.broadcasted_iota(jnp.int32, (CHUNK, 128), 1)

    def lanes_for(n):
        return lax.broadcasted_iota(jnp.int32, (n, 128), 1)

    plans[0] = jnp.zeros((8, 128), jnp.int32)
    plans[0, 0:STEPS, 0:LOOPS] = plan_ref[...]
    bext[1, 8:16, :] = bore_ref[...]
    for n, (a, b) in enumerate(around):
        @pl.when(has(a, b))
        def _():
            pltpu.make_async_remote_copy(
                src_ref=bore_ref, dst_ref=bext.at[1 - b, pl.ds(8 * (1 - a), 8), :],
                send_sem=bore_send.at[n], recv_sem=bore_recv.at[n],
                device_id={"gx": gx + a, "gy": gy + b}, device_id_type=MESH,
            ).start()
    for s in range(1, slots):
        @pl.when(tm + 2 * s < slices)
        def _():
            pltpu.make_async_remote_copy(
                src_ref=plans.at[0], dst_ref=plans.at[s],
                send_sem=plan_send.at[s], recv_sem=plan_recv.at[s],
                device_id={"tm": tm + 2 * s}, device_id_type=MESH,
            ).start()

    def halo_copy(e, at, n, a, b):
        rows = pl.ds(LOW, NYL) if b == 0 else pl.ds(LOW, 8) if b < 0 else pl.ds(HIGH - 8, 8)
        if a == 0:
            dst = hbuf.at[e, 1 if b < 0 else 0]
        else:
            at_rows = pl.ds(8, NYL) if b == 0 else pl.ds(8 + NYL, 8) if b < 0 else pl.ds(0, 8)
            dst = xbuf.at[e, 1 if a < 0 else 0, :, at_rows, :]
        return pltpu.make_async_remote_copy(
            src_ref=pool.at[at, pl.ds(OWN, HALF), rows, :], dst_ref=dst,
            send_sem=halo_send.at[e, n], recv_sem=halo_recv.at[e, n],
            device_id={"gx": gx + a, "gy": gy + b}, device_id_type=MESH,
        )

    def halo_start(e, at):
        for n, (a, b) in enumerate(around):
            @pl.when(has(a, b))
            def _():
                halo_copy(e, at, n, a, b).start()
        pending.append((e, at))

    def halo_wait(e, at):
        for n, (a, b) in enumerate(around):
            @pl.when(has(-a, -b))
            def _():
                halo_copy(e, at, n, a, b).wait_recv()

    left, right, down, up = gx > 0, gx < nx - 1, gy > 0, gy < ny - 1

    def edge_flag(r):
        return down if r < LOW else up if r >= HIGH else None

    def halo_build(e, at):
        def outer(m, crossed):
            for r, n in chunks(*ALL_ROWS):
                low = lanes_for(n) < NZ
                row = pl.ds(r - 8, n)
                q = (OWN - 1 - m) if crossed else m + 1
                one, two = xbuf[e, 0, q, row, :], xbuf[e, 1, q, row, :]
                from_left, from_right = (~low if crossed else low) & left, (low if crossed else ~low) & right
                if (r < LOW or r >= HIGH) and n == 8:
                    from_left, from_right = from_left & edge_flag(r), from_right & edge_flag(r)
                elif n > 8:
                    at_row = lax.broadcasted_iota(jnp.int32, (n, 128), 0) + r
                    inside = ((at_row >= LOW) | down) & ((at_row < HIGH) | up)
                    from_left, from_right = from_left & inside, from_right & inside
                value = jnp.where(from_left, one, jnp.where(from_right, two, f32(0.0)))
                if crossed:
                    value = pltpu.roll(value, NZ, 1)
                pool[at, m, pl.ds(r, n), :] = value

        def straight_row(m, _):
            outer(m, False)
            return _

        def crossed_row(m, _):
            outer(m, True)
            return _

        lax.fori_loop(0, HALF - 1, straight_row, 0)
        lax.fori_loop(HALF - 1, REACH, crossed_row, 0)
        for q in range(HALF):
            pool[at, OWN + q, LOW - 8:LOW, :] = jnp.where(down, hbuf[e, 0, q], f32(0.0))
            pool[at, OWN + q, HIGH:HIGH + 8, :] = jnp.where(up, hbuf[e, 1, q], f32(0.0))

    def to_wide(which, at):
        for q in range(HALF):
            top = nat[which, pl.ds(q, NZ, stride=NXL), :]
            low = nat[which, pl.ds(NXL - 1 - q, NZ, stride=NXL), :]
            pool[at, OWN + q, LOW:HIGH, :] = jnp.concatenate([top, low], axis=0).T

    load_cap.wait()
    to_wide(0, INV)
    halo_start(0, INV)
    load_init.wait()
    to_wide(1, U0)
    halo_start(1, U0)

    def clear(p, _):
        def row(m, __):
            pool[p, m, 0:8, :] = jnp.zeros((8, 128), f32)
            pool[p, m, ROWS - 8:ROWS, :] = jnp.zeros((8, 128), f32)
            return __
        return lax.fori_loop(0, WIDE, row, _)

    lax.fori_loop(0, ZX + 1, clear, 0)

    for sy in range(3):
        for sx in range(3):
            if (sx, sy) != (1, 1):
                @pl.when(~has(sx - 1, sy - 1))
                def _():
                    bext[sy, 8 * sx:8 * sx + 8, :] = jnp.full((8, 128), LOOPS, jnp.int32)
    for n, (a, b) in enumerate(around):
        @pl.when(has(-a, -b))
        def _():
            pltpu.make_async_remote_copy(
                src_ref=bore_ref, dst_ref=bext.at[1 - b, pl.ds(8 * (1 - a), 8), :],
                send_sem=bore_send.at[n], recv_sem=bore_recv.at[n],
                device_id={"gx": gx - a, "gy": gy - b}, device_id_type=MESH,
            ).wait_recv()
    for s in range(1, slots):
        @pl.when(tm - 2 * s >= 0)
        def _():
            pltpu.make_async_remote_copy(
                src_ref=plans.at[0], dst_ref=plans.at[s],
                send_sem=plan_send.at[s], recv_sem=plan_recv.at[s],
                device_id={"tm": tm - 2 * s}, device_id_type=MESH,
            ).wait_recv()

        @pl.when(tm - 2 * s < 0)
        def _():
            plans[s] = plans[0]

    SPAN = NYL + 16
    for s in range(slots):
        table = plans[s].astype(f32) - 3.5
        for n in range(STEPS):
            at_row = (s * STEPS + n) * SPAN
            for sy in range(3):
                loops = bext[sy]
                rate = jnp.zeros((24, 128), f32)
                for v in range(LOOPS):
                    rate = jnp.where(loops == v, jnp.broadcast_to(table[n:n + 1, v:v + 1], (24, 128)), rate)
                turned = jnp.concatenate([rate, jnp.zeros((104, 128), f32)], axis=0).T
                if sy == 0:
                    rates[at_row:at_row + 8, :] = turned[120:128, :]
                elif sy == 1:
                    rates[at_row + 8:at_row + 8 + NYL, :] = turned
                else:
                    rates[at_row + 8 + NYL:at_row + SPAN, :] = turned[0:8, :]
    depth = jnp.concatenate([prof_ref[...], prof_ref[...]], axis=1)

    def spread(m, _):
        here = m - REACH + NXL
        there = NXL - 1 - (m - REACH) + NXL
        pick_row = lax.broadcasted_iota(jnp.int32, (128, 128), 0)
        pick_lane = lax.broadcasted_iota(jnp.int32, (128, 128), 1)
        pick = jnp.where(pick_row == jnp.where(pick_lane < NZ, here, there), f32(1.0), f32(0.0))
        for q in range(slots * STEPS):
            part = rates[q * SPAN:(q + 1) * SPAN, :].astype(jnp.bfloat16)
            wide = jnp.dot(part, pick.astype(jnp.bfloat16), preferred_element_type=f32)
            src[m, q * SPAN:(q + 1) * SPAN, :] = wide * depth
        return _

    lax.fori_loop(1, WIDE, spread, 0)

    def beside(at, m, r, n, last):
        z_lane = lanes_for(n) & (NZ - 1)
        mid = pool[at, m, pl.ds(r, n), :]
        rows = pool[at, m - 1, pl.ds(r, n), :]
        rows = rows + (pltpu.roll(mid, NZ, 1) if last else pool[at, m + 1, pl.ds(r, n), :])
        cols = pool[at, m, pl.ds(r - 1, n), :] + pool[at, m, pl.ds(r + 1, n), :]
        above = jnp.where(z_lane != 0, pltpu.roll(mid, 1, 1), f32(0.0))
        below = jnp.where(z_lane != NZ - 1, pltpu.roll(mid, 127, 1), f32(0.0))
        return mid, (rows + cols) + (above + below)

    def sweep(first, body):
        def step(m, _):
            body(m, False)
            return _
        lax.fori_loop(first, LAST, step, 0)
        body(LAST, True)

    def sweep_sum(first, body, count):
        def halo(m, _):
            body(m, False, None)
            return _
        if first < OWN:
            lax.fori_loop(first, OWN, halo, 0)
        def own(m, totals):
            return body(m, False, totals)
        totals = tuple(jnp.zeros((CHUNK if CHUNK == 8 else NYL, 128), f32) for _ in range(count))
        totals = lax.fori_loop(OWN, LAST, own, totals)
        return body(LAST, True, totals)

    def is_own(r):
        return LOW <= r < HIGH

    def row_chunks(totals):
        if totals is None:
            return chunks(*ALL_ROWS)
        return [(LOW - 8, 8)] + chunks(*OWN_ROWS) + [(HIGH, 8)]

    halo_wait(0, INV)
    halo_build(0, INV)

    def invert(m, _):
        for r, n in chunks(*ALL_ROWS):
            cap = pool[INV, m, pl.ds(r, n), :]
            inside = cap > 0.0
            pool[DINV, m, pl.ds(r, n), :] = jnp.where(inside, 1.0 / (cap * f32(inv_step) + 6.0), f32(0.0))
            pool[CA, m, pl.ds(r, n), :] = jnp.where(inside, 1.0 / cap, f32(0.0))
        return _

    lax.fori_loop(0, WIDE, invert, 0)
    halo_wait(1, U0)
    halo_build(1, U0)

    def initial_image(m, last):
        for r, n in chunks(*ALL_ROWS):
            mid, total = beside(U0, m, r, n, last)
            pool[KU, m, pl.ds(r, n), :] = 6.0 * mid - total

    sweep(1, initial_image)

    def krylov(n_step, s, first):
        v = V + 3 * s
        flag = jnp.where(tm - 2 * s == 0, f32(1.0), f32(0.0))
        base = (s * STEPS + n_step) * SPAN

        def start(m, last, totals):
            for r, n in row_chunks(totals):
                source = src[m, pl.ds(pl.multiple_of(base, 8) + (r - 8), n), :]
                if n_step == 0:
                    residual = source - flag * pool[KU, m, pl.ds(r, n), :]
                else:
                    mid, total = beside(X + s, m, r, n, last)
                    residual = source - (6.0 * mid - total)
                z = pool[DINV, m, pl.ds(r, n), :] * residual
                pool[v, m, pl.ds(r, n), :] = z
                if totals is not None and is_own(r):
                    totals = (totals[0] + residual * z,)
            return totals

        def power(at, m, last, totals):
            for r, n in row_chunks(totals):
                mid, total = beside(at, m, r, n, last)
                z = pool[DINV, m, pl.ds(r, n), :] * total
                pool[at + 1, m, pl.ds(r, n), :] = z
                if totals is not None and is_own(r):
                    totals = (totals[0] + mid * total, totals[1] + z * total)
            return totals

        def final(m, last, totals):
            for r, n in chunks(*OWN_ROWS):
                mid, total = beside(v + 2, m, r, n, last)
                totals = (totals[0] + mid * total,)
            return totals

        sums = list(sweep_sum(first, start, 1))
        sums += sweep_sum(first + 1, functools.partial(power, v), 2)
        sums += sweep_sum(first + 2, functools.partial(power, v + 1), 2)
        sums += sweep_sum(OWN, final, 1)
        for j, total in enumerate(sums):
            mom[n_step, j, pl.ds(s, 1), :] = jnp.sum(total, axis=0, keepdims=True)

    def total_over_tiles(n_step):
        packed = jnp.zeros((8, 128), f32)
        for j in range(6):
            packed = jnp.where(lane == j, jnp.sum(mom[n_step, j], axis=1, keepdims=True), packed)
        for stage, (axis, count, me, buf) in enumerate((("gx", nx, gx, sums_x), ("gy", ny, gy, sums_y))):
            pay[n_step, stage] = packed
            copies = []
            for d in range(1, count):
                copies.append(pltpu.make_async_remote_copy(
                    src_ref=pay.at[n_step, stage], dst_ref=buf.at[n_step, d],
                    send_sem=sum_send.at[n_step, stage, d], recv_sem=sum_recv.at[n_step, stage, d],
                    device_id={axis: lax.rem(me + d, count)}, device_id_type=MESH,
                ))
                copies[-1].start()
            for d, copy in enumerate(copies):
                copy.wait_recv()
                packed = packed + buf[n_step, d + 1]
            for copy in copies:
                copy.wait_send()
        return [jnp.broadcast_to(packed[:, j:j + 1], (8, 128)) for j in range(6)]

    def cg_coefficients(mu):
        def inner(p, q, m):
            total = None
            for i, a in enumerate(p):
                for j, b in enumerate(q):
                    term = a * b * m[i + j]
                    total = term if total is None else total + term
            return total

        gap = [mu[j] - mu[j + 1] for j in range(5)]
        one = jnp.ones((8, 128), f32)
        x = [jnp.zeros((8, 128), f32)] * 3
        z, direction = [one], [one]
        inner_now = mu[0]
        for it in range(3):
            step = inner_now / inner(direction, direction, gap)
            x = [x[i] + step * direction[i] if i < len(direction) else x[i] for i in range(3)]
            if it < 2:
                grown = direction + [jnp.zeros((8, 128), f32)]
                shifted = [jnp.zeros((8, 128), f32)] + direction
                z = [(z[i] if i < len(z) else 0.0) - step * (grown[i] - shifted[i]) for i in range(len(grown))]
                inner_next = inner(z, z, mu)
                ratio = inner_next / inner_now
                direction = [z[i] + ratio * direction[i] if i < len(direction) else z[i] for i in range(len(z))]
                inner_now = inner_next
        return x

    for n_step, first in ((0, 1), (1, 4)):
        def each(s, _):
            krylov(n_step, s, first)
            return _

        mom[n_step] = jnp.zeros((6, 8, 128), f32)
        lax.fori_loop(0, slots, each, 0)
        weights = cg_coefficients(total_over_tiles(n_step))
        for i in range(3):
            coef[n_step, i] = weights[i]

        def update(s, _):
            w = [coef[n_step, i, pl.ds(s, 1), :] for i in range(3)]
            flag = jnp.where(tm - 2 * s == 0, f32(1.0), f32(0.0))

            def row(m, _):
                for r, n in chunks(*(ALL_ROWS if n_step == 0 else OWN_ROWS)):
                    value = w[0] * pool[V + 3 * s, m, pl.ds(r, n), :]
                    value = value + w[1] * pool[V + 3 * s + 1, m, pl.ds(r, n), :]
                    value = value + w[2] * pool[V + 3 * s + 2, m, pl.ds(r, n), :]
                    if n_step == 0:
                        value = value + flag * pool[U0, m, pl.ds(r, n), :]
                    else:
                        value = jnp.where(tm - 2 * s >= 0, value + pool[X + s, m, pl.ds(r, n), :], f32(0.0))
                    pool[X + s, m, pl.ds(r, n), :] = value
                return _

            return lax.fori_loop(3 if n_step == 0 else OWN, WIDE, row, _)

        lax.fori_loop(0, slots, update, 0)

    def shift_factors(scale):
        def row(m, _):
            for r, n in chunks(*ALL_ROWS):
                a = pool[KU, m, pl.ds(r, n), :] * f32(2.0 * scale)
                pool[CA, m, pl.ds(r, n), :] = a
                pool[CG, m, pl.ds(r, n), :] = 6.0 * a - 2.0
            return _
        lax.fori_loop(0, WIDE, row, 0)

    def keep(m, _):
        for r, n in chunks(*ALL_ROWS):
            pool[KU, m, pl.ds(r, n), :] = pool[CA, m, pl.ds(r, n), :]
        return _

    lax.fori_loop(0, WIDE, keep, 0)

    def propagate(at, to):
        def first_term(m, last):
            for r, n in chunks(*ALL_ROWS):
                mid, total = beside(at, m, r, n, last)
                pool[TS, m, pl.ds(r, n), :] = 0.5 * (pool[CG, m, pl.ds(r, n), :] * mid - pool[CA, m, pl.ds(r, n), :] * total)

        def term(before, now, m, last, rows):
            out = []
            for r, n in chunks(*rows):
                mid, total = beside(now, m, r, n, last)
                out.append((r, n, mid, pool[CG, m, pl.ds(r, n), :] * mid - pool[CA, m, pl.ds(r, n), :] * total
                            - pool[before, m, pl.ds(r, n), :]))
            return out

        def store(before, now, into, m, last):
            for r, n in chunks(*ALL_ROWS):
                mid, total = beside(now, m, r, n, last)
                pool[into, m, pl.ds(r, n), :] = (
                    pool[CG, m, pl.ds(r, n), :] * mid - pool[CA, m, pl.ds(r, n), :] * total
                    - pool[before, m, pl.ds(r, n), :])

        def add_up(m, last):
            for r, n in chunks(*OWN_ROWS):
                mid, total = beside(TS + 5, m, r, n, last)
                final = pool[CG, m, pl.ds(r, n), :] * mid - pool[CA, m, pl.ds(r, n), :] * total - pool[TS + 4, m, pl.ds(r, n), :]
                value = f32(cheb[0]) * pool[at, m, pl.ds(r, n), :] + f32(cheb[7]) * final + f32(cheb[6]) * mid
                for j in range(1, 6):
                    value = value + f32(cheb[j]) * pool[TS + j - 1, m, pl.ds(r, n), :]
                pool[to, m, pl.ds(r, n), :] = pool[to, m, pl.ds(r, n), :] + value

        sweep(1, first_term)
        sweep(2, functools.partial(store, at, TS, TS + 1))

        def later(j, _):
            sweep(j, functools.partial(store, TS + j - 3, TS + j - 2, TS + j - 1))
            return _

        lax.fori_loop(3, 7, later, 0)
        sweep(OWN, add_up)

    scale_one = 1.0 / (12.0 * slices)
    e = 2
    started = {}

    def start_slot(s):
        nonlocal e
        halo_start(e, X + s)
        started[s] = e
        e += 1

    span = slots // 2
    ready = {}
    while span >= 1:
        todo = [s for s in range(slots - 1, -1, -1) if s >= span and s < 2 * span]
        for s in todo:
            if s not in started:
                start_slot(s)
        shift_factors(2 * span * scale_one)
        for s in todo:
            halo_wait(started[s], X + s)
            halo_build(started[s], X + s)
            propagate(X + s, X + s - span)
            if s - span >= span // 2 and s - span < span and span > 1 and s - span > 0:
                start_slot(s - span)
        span //= 2

    shift = pltpu.make_async_remote_copy(
        src_ref=pool.at[X, pl.ds(OWN, HALF), pl.ds(LOW, NYL), :],
        dst_ref=pool.at[ZX, pl.ds(OWN, HALF), pl.ds(LOW, NYL), :],
        send_sem=shift_send.at[0], recv_sem=shift_recv.at[0],
        device_id={"tm": lax.rem(tm + 1, slices)}, device_id_type=MESH,
    )

    @pl.when(tm < slices - 1)
    def _():
        shift.start()

    shift_factors(scale_one)

    @pl.when(tm > 0)
    def _():
        shift.wait_recv()

    @pl.when(tm == 0)
    def _():
        pool[ZX, OWN:WIDE, LOW:HIGH, :] = jnp.zeros((HALF, NYL, 128), f32)

    halo_start(e, ZX)
    halo_wait(e, ZX)
    halo_build(e, ZX)

    @pl.when(tm < slices - 1)
    def _():
        shift.wait_send()

    propagate(ZX, X)

    for q in range(HALF):
        turned = pool[X, OWN + q, LOW:HIGH, :].T
        nat[1, pl.ds(q, NZ, stride=NXL), :] = turned[0:NZ, :]
        nat[1, pl.ds(NXL - 1 - q, NZ, stride=NXL), :] = turned[NZ:2 * NZ, :]
    store_out = pltpu.make_async_copy(nat.at[1], out_ref, load_sem.at[2])
    store_out.start()

    for n, (a, b) in enumerate(around):
        @pl.when(has(a, b))
        def _():
            pltpu.make_async_remote_copy(
                src_ref=bore_ref, dst_ref=bext.at[1 - b, pl.ds(8 * (1 - a), 8), :],
                send_sem=bore_send.at[n], recv_sem=bore_recv.at[n],
                device_id={"gx": gx + a, "gy": gy + b}, device_id_type=MESH,
            ).wait_send()
            for e_done, at in pending:
                halo_copy(e_done, at, n, a, b).wait_send()
    for s in range(1, slots):
        @pl.when(tm + 2 * s < slices)
        def _():
            pltpu.make_async_remote_copy(
                src_ref=plans.at[0], dst_ref=plans.at[s],
                send_sem=plan_send.at[s], recv_sem=plan_recv.at[s],
                device_id={"tm": tm + 2 * s}, device_id_type=MESH,
            ).wait_send()
    store_out.wait()


def per_device(sizes, initial, capacity, profile, bore_loop, plan):
    slices = sizes[0]
    slots = max(1, slices // 2)
    exchanges = 2 + (slots - 1) + 1
    pool_size = 6 + slots + max(3 * slots, TERMS - 1) + 1
    f32 = jnp.float32
    dma = pltpu.SemaphoreType.DMA
    out = pl.pallas_call(
        functools.partial(kernel, sizes),
        out_shape=jax.ShapeDtypeStruct((NZ * NXL, NYL), f32),
        in_specs=[
            pl.BlockSpec(memory_space=pl.ANY),
            pl.BlockSpec(memory_space=pl.ANY),
            pl.BlockSpec(memory_space=pltpu.VMEM),
            pl.BlockSpec(memory_space=pltpu.VMEM),
            pl.BlockSpec(memory_space=pltpu.VMEM),
        ],
        out_specs=pl.BlockSpec(memory_space=pl.ANY),
        scratch_shapes=[
            pltpu.VMEM((2, NZ * NXL, NYL), f32),
            pltpu.VMEM((pool_size, WIDE, ROWS, 128), f32),
            pltpu.VMEM((WIDE, slots * STEPS * (NYL + 16), 128), f32),
            pltpu.VMEM((exchanges, 2, HALF, NYL + 16, 128), f32),
            pltpu.VMEM((exchanges, 2, HALF, 8, 128), f32),
            pltpu.VMEM((3, 24, 128), jnp.int32),
            pltpu.VMEM((slots, 8, 128), jnp.int32),
            pltpu.VMEM((slots * STEPS * (NYL + 16), 128), f32),
            pltpu.VMEM((STEPS, 6, 8, 128), f32),
            pltpu.VMEM((STEPS, 2, 8, 128), f32),
            pltpu.VMEM((STEPS, 3, 8, 128), f32),
            pltpu.VMEM((STEPS, 8, 8, 128), f32),
            pltpu.VMEM((STEPS, 8, 8, 128), f32),
            dma((3,)),
            dma((8,)),
            dma((8,)),
            dma((slots,)),
            dma((slots,)),
            dma((exchanges, 8)),
            dma((exchanges, 8)),
            dma((STEPS, 2, 8)),
            dma((STEPS, 2, 8)),
            dma((1,)),
            dma((1,)),
        ],
        compiler_params=pltpu.CompilerParams(
            collective_id=0, has_side_effects=True, vmem_limit_bytes=56 * 1024 * 1024
        ),
    )(
        initial.reshape(NZ * NXL, NYL),
        capacity.reshape(NZ * NXL, NYL),
        profile.reshape(1, NZ),
        bore_loop,
        plan[0],
    )
    return out.reshape(1, NZ, NXL, NYL)


def solution(mesh):
    sizes = (mesh.shape["tm"], mesh.shape["gx"], mesh.shape["gy"])
    return jax.shard_map(
        functools.partial(per_device, sizes),
        mesh=mesh,
        in_specs=(
            P(None, "gx", "gy"),
            P(None, "gx", "gy"),
            P(),
            P("gx", "gy"),
            P("tm", None, None),
        ),
        out_specs=P("tm", None, "gx", "gy"),
        check_vma=False,
    )
```

time: 2090 us -> 171 us (0.08)
  the two profiles are of different devices: /device:TPU:161 before, /device:TPU:73 now
where the time goes in v1:
time: 171 us
  Pallas kernels  169 us (99%)
    pallas_call x1, Pallas kernels, per_device(): pl.pallas_call(functools.partial(kernel, sizes), out_shape=jax.ShapeDtype...  169 us

profile of v1, /device:TPU:73, one launch (start us, length us, event | category | flops | bytes accessed | tf_op | source)
XLA Modules:
  0.0 171.0 jit_solution(1117396409119397465)
XLA Ops:
  0.0 169.4 %shard_map.55 = f32[512,128]{1,0:T(8,128)} custom-call(f32[512,128]{1,0:T(8,128)} %bitcast.6, f32[512,128]{1,0:T(8,128)} %bitcast.7, f32[1,64]{1,0:T(1,128)} %bitcast.9, s32[8,128]{1,0:T(8,128)} %bore_ref.1, s32[2,16]{1,0:T(2,128)} %bitcast.8), custom_call_target="tpu_custom_call" | custom-call | tf_op jit(solution)/shard_map/pallas_call | solution.py:605
  169.4 1.7 copy.7

commit v2 on v1

v2 whole, which is shorter than its diff:
```python
import functools

import jax
import jax.numpy as jnp
import numpy as np
from jax import lax
from jax.experimental import pallas as pl
from jax.experimental.pallas import tpu as pltpu
from jax.sharding import PartitionSpec as P

MESH = pl.DeviceIdType.MESH
STEPS = 2
TERMS = 8
LOOPS = 16
HORIZON = 4.0 / 3.0
EXPONENT = 16.0

NZ, NXL, NYL = 64, 8, 128
HALF = NXL // 2
REACH = TERMS - 1
OWN = REACH
WIDE = REACH + HALF
LAST = WIDE - 1
ROWS = NYL + 32
LOW, HIGH = 16, 16 + NYL
CHUNK = 16


def cheb_coeffs(term_count):
    angles = np.pi * (np.arange(term_count) + 0.5) / term_count
    cheb_nodes = np.cos(angles)
    samples = np.exp(-EXPONENT * (cheb_nodes + 1.0))
    coeffs = [
        2.0 / term_count * float(np.sum(samples * np.cos(term_index * angles)))
        for term_index in range(term_count)
    ]
    coeffs[0] = coeffs[0] / 2.0
    return coeffs


def chunks(low, high, size):
    return [(r, min(size, high - r)) for r in range(low, high, size)]


def kernel(
    sizes,
    init_hbm, cap_hbm, prof_ref, bore_ref, plan_ref, out_ref,
    nat, src, xbuf, hbuf, bext, plans, rates, mom, pay, coef, sums_x, sums_y,
    load_sem, bore_send, bore_recv, plan_send, plan_recv, halo_send, halo_recv,
    sum_send, sum_recv, shift_send, shift_recv,
    heat, inv, dinv, u0, ku, ca, cg, xs, v0s, v1s, v2s, *ts,
):
    slices, nx, ny = sizes
    slots = max(1, slices // 2)
    inv_step = STEPS * slices / HORIZON
    tm, gx, gy = lax.axis_index("tm"), lax.axis_index("gx"), lax.axis_index("gy")
    f32 = jnp.float32
    cheb = cheb_coeffs(TERMS)

    def has(a, b):
        x, y = gx + a, gy + b
        return (x >= 0) & (x < nx) & (y >= 0) & (y < ny)

    around = [(a, b) for b in (-1, 0, 1) for a in (-1, 0, 1) if (a, b) != (0, 0)]
    around.sort(key=lambda ab: ab[1] == 0)

    load_cap = pltpu.make_async_copy(cap_hbm, nat.at[0], load_sem.at[0])
    load_init = pltpu.make_async_copy(init_hbm, nat.at[1], load_sem.at[1])
    load_cap.start()
    load_init.start()

    barrier = pltpu.get_barrier_semaphore()
    for d in range(1, nx):
        pl.semaphore_signal(barrier, inc=1, device_id={"gx": lax.rem(gx + d, nx)}, device_id_type=MESH)
    for d in range(1, ny):
        pl.semaphore_signal(barrier, inc=1, device_id={"gy": lax.rem(gy + d, ny)}, device_id_type=MESH)
    for a, b in around:
        if a and b:
            @pl.when(has(a, b))
            def _():
                pl.semaphore_signal(barrier, inc=1, device_id={"gx": gx + a, "gy": gy + b}, device_id_type=MESH)
    spans = [1] + [2 * s for s in range(1, slots)]
    for s in spans:
        @pl.when(tm >= s)
        def _():
            pl.semaphore_signal(barrier, inc=1, device_id={"tm": tm - s}, device_id_type=MESH)
    greeted = nx - 1 + ny - 1
    for a, b in around:
        if a and b:
            greeted = greeted + jnp.where(has(a, b), 1, 0)
    for s in spans:
        greeted = greeted + jnp.where(tm + s < slices, 1, 0)
    pl.semaphore_wait(barrier, greeted)

    lane = lax.broadcasted_iota(jnp.int32, (8, 128), 1)

    plans[0] = jnp.zeros((8, 128), jnp.int32)
    plans[0, 0:STEPS, 0:LOOPS] = plan_ref[...]
    bext[1, 8:16, :] = bore_ref[...]
    for n, (a, b) in enumerate(around):
        @pl.when(has(a, b))
        def _():
            pltpu.make_async_remote_copy(
                src_ref=bore_ref, dst_ref=bext.at[1 - b, pl.ds(8 * (1 - a), 8), :],
                send_sem=bore_send.at[n], recv_sem=bore_recv.at[n],
                device_id={"gx": gx + a, "gy": gy + b}, device_id_type=MESH,
            ).start()
    for s in range(1, slots):
        @pl.when(tm + 2 * s < slices)
        def _():
            pltpu.make_async_remote_copy(
                src_ref=plans.at[0], dst_ref=plans.at[s],
                send_sem=plan_send.at[s], recv_sem=plan_recv.at[s],
                device_id={"tm": tm + 2 * s}, device_id_type=MESH,
            ).start()

    def halo_copy(e, at, n, a, b):
        rows = pl.ds(LOW, NYL) if b == 0 else pl.ds(LOW, 8) if b < 0 else pl.ds(HIGH - 8, 8)
        if a == 0:
            dst = hbuf.at[e, 1 if b < 0 else 0]
        else:
            at_rows = pl.ds(8, NYL) if b == 0 else pl.ds(8 + NYL, 8) if b < 0 else pl.ds(0, 8)
            dst = xbuf.at[e, 1 if a < 0 else 0, :, at_rows, :]
        return pltpu.make_async_remote_copy(
            src_ref=at.at[pl.ds(OWN, HALF), rows, :], dst_ref=dst,
            send_sem=halo_send.at[e, n], recv_sem=halo_recv.at[e, n],
            device_id={"gx": gx + a, "gy": gy + b}, device_id_type=MESH,
        )

    def halo_start(e, at):
        for n, (a, b) in enumerate(around):
            @pl.when(has(a, b))
            def _():
                halo_copy(e, at, n, a, b).start()

    def halo_wait(e, at):
        for n, (a, b) in enumerate(around):
            @pl.when(has(-a, -b))
            def _():
                halo_copy(e, at, n, a, b).wait_recv()

    left, right, down, up = gx > 0, gx < nx - 1, gy > 0, gy < ny - 1

    low_lanes = lax.broadcasted_iota(jnp.int32, (1, 8, 128), 2) < NZ

    def halo_build(e, at):
        for r, n in [(0, 8), (8, NYL), (8 + NYL, 8)]:
            edge = down if r == 0 else up if r > 8 else True
            for crossed in (False, True):
                from_left = (~low_lanes if crossed else low_lanes) & left & edge
                from_right = (low_lanes if crossed else ~low_lanes) & right & edge
                for m in range(HALF - 1, REACH) if crossed else range(HALF - 1):
                    q = REACH - 1 - m if crossed else m + 1
                    one = xbuf[e, 0, q, r:r + n, :].reshape(n // 8, 8, 128)
                    two = xbuf[e, 1, q, r:r + n, :].reshape(n // 8, 8, 128)
                    value = jnp.where(from_left, one, jnp.where(from_right, two, f32(0.0)))
                    if crossed:
                        value = pltpu.roll(value, NZ, 2)
                    at[m, LOW - 8 + r:LOW - 8 + r + n, :] = value.reshape(n, 128)
        at[OWN:WIDE, LOW - 8:LOW, :] = jnp.where(down, hbuf[e, 0], f32(0.0))
        at[OWN:WIDE, HIGH:HIGH + 8, :] = jnp.where(up, hbuf[e, 1], f32(0.0))

    def to_wide(which, at):
        for q in range(HALF):
            top = nat[which, pl.ds(q, NZ, stride=NXL), :]
            low = nat[which, pl.ds(NXL - 1 - q, NZ, stride=NXL), :]
            at[OWN + q, LOW:HIGH, :] = jnp.concatenate([top, low], axis=0).T

    load_cap.wait()
    to_wide(0, heat)
    halo_start(0, heat)
    load_init.wait()
    to_wide(1, u0)
    halo_start(1, u0)

    for sy in range(3):
        for sx in range(3):
            if (sx, sy) != (1, 1):
                @pl.when(~has(sx - 1, sy - 1))
                def _():
                    bext[sy, 8 * sx:8 * sx + 8, :] = jnp.full((8, 128), LOOPS, jnp.int32)
    for n, (a, b) in enumerate(around):
        @pl.when(has(-a, -b))
        def _():
            pltpu.make_async_remote_copy(
                src_ref=bore_ref, dst_ref=bext.at[1 - b, pl.ds(8 * (1 - a), 8), :],
                send_sem=bore_send.at[n], recv_sem=bore_recv.at[n],
                device_id={"gx": gx - a, "gy": gy - b}, device_id_type=MESH,
            ).wait_recv()
    for s in range(1, slots):
        @pl.when(tm - 2 * s >= 0)
        def _():
            pltpu.make_async_remote_copy(
                src_ref=plans.at[0], dst_ref=plans.at[s],
                send_sem=plan_send.at[s], recv_sem=plan_recv.at[s],
                device_id={"tm": tm - 2 * s}, device_id_type=MESH,
            ).wait_recv()

        @pl.when(tm - 2 * s < 0)
        def _():
            plans[s] = plans[0]

    SPAN = NYL + 16
    loops = jnp.concatenate([bext[0], bext[1], bext[2]], axis=0)
    for s in range(slots):
        table = plans[s].astype(f32) - 3.5
        for n in range(STEPS):
            at_row = (s * STEPS + n) * SPAN
            rate = jnp.zeros((72, 128), f32)
            for v in range(LOOPS):
                rate = jnp.where(loops == v, jnp.broadcast_to(table[n:n + 1, v:v + 1], (72, 128)), rate)
            turned = jnp.concatenate([rate, jnp.zeros((56, 128), f32)], axis=0).T
            rates[at_row:at_row + 8, :] = pltpu.roll(turned[120:128, :], 24, 1)
            rates[at_row + 8:at_row + 8 + NYL, :] = turned
            rates[at_row + 8 + NYL:at_row + SPAN, :] = pltpu.roll(turned[0:8, :], 104, 1)
    depth = jnp.concatenate([prof_ref[...], prof_ref[...]], axis=1)

    def spread(m, _):
        here = 32 + m - REACH
        there = 32 + NXL - 1 - (m - REACH)
        pick_row = lax.broadcasted_iota(jnp.int32, (128, 128), 0)
        pick_lane = lax.broadcasted_iota(jnp.int32, (128, 128), 1)
        pick = jnp.where(pick_row == jnp.where(pick_lane < NZ, here, there), f32(1.0), f32(0.0)).astype(jnp.bfloat16)
        wide = jnp.dot(rates[...].astype(jnp.bfloat16), pick, preferred_element_type=f32)
        src[m] = wide * depth
        return _

    lax.fori_loop(1, WIDE, spread, 0)

    def rolled(value, by):
        return pltpu.roll(value, by, 2)

    def beside(at, first, r, n):
        count = WIDE - first
        mid = at[first:WIDE, r:r + n, :]
        before = jnp.concatenate([at[first - 1:first, r:r + n, :], mid[:-1]], axis=0) if count > 1 else at[first - 1:first, r:r + n, :]
        across = rolled(mid[-1:], NZ)
        after = jnp.concatenate([mid[1:], across], axis=0) if count > 1 else across
        cols = at[first:WIDE, r - 1:r - 1 + n, :] + at[first:WIDE, r + 1:r + 1 + n, :]
        z_lane = lax.broadcasted_iota(jnp.int32, (count, n, 128), 2) & (NZ - 1)
        above = jnp.where(z_lane != 0, rolled(mid, 1), f32(0.0))
        below = jnp.where(z_lane != NZ - 1, rolled(mid, 127), f32(0.0))
        return mid, ((before + after) + cols) + (above + below)

    def blocks(first, wide):
        return chunks(LOW - 8, HIGH + 8, CHUNK) if wide else chunks(LOW, HIGH, CHUNK)

    def add_own(total, value, first, r, n):
        value = value[OWN - first:]
        low, high = max(LOW - r, 0), min(HIGH - r, n)
        if high <= low:
            return total
        value = value[:, low:high, :]
        return total + jnp.sum(value.reshape(-1, 8, 128), axis=0)

    halo_wait(0, heat)
    halo_build(0, heat)

    for r, n in chunks(LOW - 8, HIGH + 8, CHUNK):
        cap = heat[:, r:r + n, :]
        inside = cap > 0.0
        dinv[:, r:r + n, :] = jnp.where(inside, 1.0 / (cap * f32(inv_step) + 6.0), f32(0.0))
        inv[:, r:r + n, :] = jnp.where(inside, 1.0 / cap, f32(0.0))

    halo_wait(1, u0)
    halo_build(1, u0)
    for r, n in blocks(1, True):
        mid, total = beside(u0, 1, r, n)
        ku[1:WIDE, r:r + n, :] = 6.0 * mid - total

    zero = jnp.zeros((8, 128), f32)

    def krylov(n_step, s, first):
        x, v0, v1, v2 = xs.at[s], v0s.at[s], v1s.at[s], v2s.at[s]
        flag = jnp.where(tm - 2 * s == 0, f32(1.0), f32(0.0))
        base = s * (STEPS * SPAN) + n_step * SPAN
        sums = [zero] * 6
        for r, n in blocks(first, True):
            residual = src[first:WIDE, pl.ds(pl.multiple_of(base + (r - 8), 8), n), :]
            if n_step == 0:
                residual = residual - flag * ku[first:WIDE, r:r + n, :]
            else:
                mid, total = beside(x, first, r, n)
                residual = residual - (6.0 * mid - total)
            z = dinv[first:WIDE, r:r + n, :] * residual
            v0[first:WIDE, r:r + n, :] = z
            sums[0] = add_own(sums[0], residual * z, first, r, n)
        for k, (now, then) in enumerate(((v0, v1), (v1, v2))):
            begin = first + 1 + k
            for r, n in blocks(begin, True):
                mid, total = beside(now, begin, r, n)
                z = dinv[begin:WIDE, r:r + n, :] * total
                then[begin:WIDE, r:r + n, :] = z
                sums[2 * k + 1] = add_own(sums[2 * k + 1], mid * total, begin, r, n)
                sums[2 * k + 2] = add_own(sums[2 * k + 2], z * total, begin, r, n)
        for r, n in blocks(OWN, False):
            mid, total = beside(v2, OWN, r, n)
            sums[5] = add_own(sums[5], mid * total, OWN, r, n)
        for j, total in enumerate(sums):
            mom[n_step, j, pl.ds(s, 1), :] = jnp.sum(total, axis=0, keepdims=True)

    def total_over_tiles(n_step):
        packed = jnp.zeros((8, 128), f32)
        for j in range(6):
            packed = jnp.where(lane == j, jnp.sum(mom[n_step, j], axis=1, keepdims=True), packed)
        for stage, (axis, count, me, buf) in enumerate((("gx", nx, gx, sums_x), ("gy", ny, gy, sums_y))):
            pay[n_step, stage] = packed
            copies = []
            for d in range(1, count):
                copies.append(pltpu.make_async_remote_copy(
                    src_ref=pay.at[n_step, stage], dst_ref=buf.at[n_step, d],
                    send_sem=sum_send.at[n_step, stage, d], recv_sem=sum_recv.at[n_step, stage, d],
                    device_id={axis: lax.rem(me + d, count)}, device_id_type=MESH,
                ))
                copies[-1].start()
            for d, copy in enumerate(copies):
                copy.wait_recv()
                packed = packed + buf[n_step, d + 1]
            for copy in copies:
                copy.wait_send()
        return [jnp.broadcast_to(packed[:, j:j + 1], (8, 128)) for j in range(6)]

    def cg_coefficients(mu):
        def inner(p, q, m):
            total = None
            for i, a in enumerate(p):
                for j, b in enumerate(q):
                    term = a * b * m[i + j]
                    total = term if total is None else total + term
            return total

        gap = [mu[j] - mu[j + 1] for j in range(5)]
        one = jnp.ones((8, 128), f32)
        x = [jnp.zeros((8, 128), f32)] * 3
        z, direction = [one], [one]
        inner_now = mu[0]
        for it in range(3):
            step = inner_now / inner(direction, direction, gap)
            x = [x[i] + step * direction[i] if i < len(direction) else x[i] for i in range(3)]
            if it < 2:
                grown = direction + [jnp.zeros((8, 128), f32)]
                shifted = [jnp.zeros((8, 128), f32)] + direction
                z = [(z[i] if i < len(z) else 0.0) - step * (grown[i] - shifted[i]) for i in range(len(grown))]
                inner_next = inner(z, z, mu)
                ratio = inner_next / inner_now
                direction = [z[i] + ratio * direction[i] if i < len(direction) else z[i] for i in range(len(z))]
                inner_now = inner_next
        return x

    for n_step, first in ((0, 1), (1, 4)):
        def each(s, _):
            krylov(n_step, s, first)
            return _

        mom[n_step] = jnp.zeros((6, 8, 128), f32)
        lax.fori_loop(0, slots, each, 0)
        weights = cg_coefficients(total_over_tiles(n_step))
        for i in range(3):
            coef[n_step, i] = weights[i]

        def update(s, _):
            w = [coef[n_step, i, pl.ds(s, 1), :].reshape(1, 1, 128) for i in range(3)]
            flag = jnp.where(tm - 2 * s == 0, f32(1.0), f32(0.0))
            begin = 3 if n_step == 0 else OWN
            for r, n in blocks(begin, n_step == 0):
                here = (s, slice(begin, WIDE), slice(r, r + n))
                value = w[0] * v0s[here] + w[1] * v1s[here] + w[2] * v2s[here]
                if n_step == 0:
                    xs[here] = value + flag * u0[begin:WIDE, r:r + n, :]
                else:
                    xs[here] = jnp.where(tm - 2 * s >= 0, value + xs[here], f32(0.0))
            return _

        lax.fori_loop(0, slots, update, 0)

    plan_rows = []
    span = slots // 2
    while span >= 1:
        for s in range(2 * span - 1, span - 1, -1):
            plan_rows.append((s, s - span, 2 * span))
        span //= 2
    plan_rows.append((slots, 0, 1))
    order = [row[0] for row in plan_rows]
    last = len(plan_rows) - 1
    finished = {s: max((p for p, row in enumerate(plan_rows) if row[1] == s), default=-1) for s in order[:-1]}

    def pick(p, values):
        out = values[-1]
        for i in range(len(values) - 2, -1, -1):
            out = jnp.where(p == i, values[i], out)
        return out

    shift = pltpu.make_async_remote_copy(
        src_ref=xs.at[0, pl.ds(OWN, HALF), pl.ds(LOW, NYL), :],
        dst_ref=xs.at[slots, pl.ds(OWN, HALF), pl.ds(LOW, NYL), :],
        send_sem=shift_send.at[0], recv_sem=shift_recv.at[0],
        device_id={"tm": lax.rem(tm + 1, slices)}, device_id_type=MESH,
    )

    def pass_on():
        @pl.when(tm < slices - 1)
        def _():
            shift.start()

        @pl.when(tm == 0)
        def _():
            xs[slots, OWN:WIDE, LOW:HIGH, :] = jnp.zeros((HALF, NYL, 128), f32)

        @pl.when(tm > 0)
        def _():
            shift.wait_recv()

        halo_start(2 + last, xs.at[slots])

        @pl.when(tm < slices - 1)
        def _():
            shift.wait_send()

    for s in order[:-1]:
        if finished[s] < 0:
            halo_start(2 + order.index(s), xs.at[s])
    if last == 0:
        pass_on()

    def combine(before, now, first, r, n):
        mid, total = beside(now, first, r, n)
        return mid, cg[first:WIDE, r:r + n, :] * mid - ca[first:WIDE, r:r + n, :] * total, before[first:WIDE, r:r + n, :] if before is not None else None

    def section(p, carry):
        at, to = pick(p, order), pick(p, [row[1] for row in plan_rows])
        factor = pick(p, [jnp.float32(2.0 * row[2] / (12.0 * slices)) for row in plan_rows])
        for r, n in chunks(LOW - 8, HIGH + 8, CHUNK):
            a = inv[:, r:r + n, :] * factor
            ca[:, r:r + n, :] = a
            cg[:, r:r + n, :] = 6.0 * a - 2.0
        ts[0][OWN:WIDE, LOW:HIGH, :] = xs[at, OWN:WIDE, LOW:HIGH, :]
        halo_wait(2 + p, xs.at[at])
        halo_build(2 + p, ts[0])
        for j in range(1, TERMS - 1):
            for r, n in blocks(j, True):
                mid, value, before = combine(ts[j - 2] if j > 1 else None, ts[j - 1], j, r, n)
                ts[j][j:WIDE, r:r + n, :] = 0.5 * value if j == 1 else value - before
        for r, n in blocks(OWN, False):
            mid, value, before = combine(ts[5], ts[6], OWN, r, n)
            value = f32(cheb[7]) * (value - before) + f32(cheb[6]) * mid + f32(cheb[5]) * before
            for j in range(5):
                value = value + f32(cheb[j]) * ts[j][OWN:WIDE, r:r + n, :]
            xs[to, OWN:WIDE, r:r + n, :] = xs[to, OWN:WIDE, r:r + n, :] + value
        for s, p_done in finished.items():
            if p_done >= 0:
                @pl.when(p == p_done)
                def _():
                    halo_start(2 + order.index(s), xs.at[s])
        if last > 0:
            @pl.when(p == last - 1)
            def _():
                pass_on()
        return carry

    lax.fori_loop(0, last + 1, section, 0)

    for q in range(HALF):
        turned = xs[0, OWN + q, LOW:HIGH, :].T
        nat[1, pl.ds(q, NZ, stride=NXL), :] = turned[0:NZ, :]
        nat[1, pl.ds(NXL - 1 - q, NZ, stride=NXL), :] = turned[NZ:2 * NZ, :]
    store_out = pltpu.make_async_copy(nat.at[1], out_ref, load_sem.at[2])
    store_out.start()

    for n, (a, b) in enumerate(around):
        @pl.when(has(a, b))
        def _():
            pltpu.make_async_remote_copy(
                src_ref=bore_ref, dst_ref=bext.at[1 - b, pl.ds(8 * (1 - a), 8), :],
                send_sem=bore_send.at[n], recv_sem=bore_recv.at[n],
                device_id={"gx": gx + a, "gy": gy + b}, device_id_type=MESH,
            ).wait_send()
            halo_copy(0, heat, n, a, b).wait_send()
            halo_copy(1, u0, n, a, b).wait_send()
            for p, s in enumerate(order):
                halo_copy(2 + p, xs.at[s], n, a, b).wait_send()
    for s in range(1, slots):
        @pl.when(tm + 2 * s < slices)
        def _():
            pltpu.make_async_remote_copy(
                src_ref=plans.at[0], dst_ref=plans.at[s],
                send_sem=plan_send.at[s], recv_sem=plan_recv.at[s],
                device_id={"tm": tm + 2 * s}, device_id_type=MESH,
            ).wait_send()
    store_out.wait()


def per_device(sizes, initial, capacity, profile, bore_loop, plan):
    slices = sizes[0]
    slots = max(1, slices // 2)
    exchanges = 2 + (slots - 1) + 1
    wide = (WIDE, ROWS, 128)
    f32 = jnp.float32
    dma = pltpu.SemaphoreType.DMA
    out = pl.pallas_call(
        functools.partial(kernel, sizes),
        out_shape=jax.ShapeDtypeStruct((NZ * NXL, NYL), f32),
        in_specs=[
            pl.BlockSpec(memory_space=pl.ANY),
            pl.BlockSpec(memory_space=pl.ANY),
            pl.BlockSpec(memory_space=pltpu.VMEM),
            pl.BlockSpec(memory_space=pltpu.VMEM),
            pl.BlockSpec(memory_space=pltpu.VMEM),
        ],
        out_specs=pl.BlockSpec(memory_space=pl.ANY),
        scratch_shapes=[
            pltpu.VMEM((2, NZ * NXL, NYL), f32),
            pltpu.VMEM((WIDE, slots * STEPS * (NYL + 16), 128), f32),
            pltpu.VMEM((exchanges, 2, HALF, NYL + 16, 128), f32),
            pltpu.VMEM((exchanges, 2, HALF, 8, 128), f32),
            pltpu.VMEM((3, 24, 128), jnp.int32),
            pltpu.VMEM((slots, 8, 128), jnp.int32),
            pltpu.VMEM((slots * STEPS * (NYL + 16), 128), f32),
            pltpu.VMEM((STEPS, 6, 8, 128), f32),
            pltpu.VMEM((STEPS, 2, 8, 128), f32),
            pltpu.VMEM((STEPS, 3, 8, 128), f32),
            pltpu.VMEM((STEPS, 8, 8, 128), f32),
            pltpu.VMEM((STEPS, 8, 8, 128), f32),
            dma((3,)),
            dma((8,)),
            dma((8,)),
            dma((slots,)),
            dma((slots,)),
            dma((exchanges, 8)),
            dma((exchanges, 8)),
            dma((STEPS, 2, 8)),
            dma((STEPS, 2, 8)),
            dma((1,)),
            dma((1,)),
        ] + [pltpu.VMEM(wide, f32)] * 7 + [pltpu.VMEM((slots + 1, *wide), f32)]
        + [pltpu.VMEM((slots, *wide), f32)] * 3 + [pltpu.VMEM(wide, f32)] * (TERMS - 1),
        compiler_params=pltpu.CompilerParams(
            collective_id=0, has_side_effects=True, vmem_limit_bytes=56 * 1024 * 1024
        ),
    )(
        initial.reshape(NZ * NXL, NYL),
        capacity.reshape(NZ * NXL, NYL),
        profile.reshape(1, NZ),
        bore_loop,
        plan[0],
    )
    return out.reshape(1, NZ, NXL, NYL)


def solution(mesh):
    sizes = (mesh.shape["tm"], mesh.shape["gx"], mesh.shape["gy"])
    return jax.shard_map(
        functools.partial(per_device, sizes),
        mesh=mesh,
        in_specs=(
            P(None, "gx", "gy"),
            P(None, "gx", "gy"),
            P(),
            P("gx", "gy"),
            P("tm", None, None),
        ),
        out_specs=P("tm", None, "gx", "gy"),
        check_vma=False,
    )
```

time: 171 us -> 80.6 us (0.47)
  the two profiles are of different devices: /device:TPU:73 before, /device:TPU:81 now
where the time goes in v2:
time: 80.6 us; the launch traced here: 80.4 us
  Pallas kernels  78.7 us (98%)
  local copies, waits for them, and re-layouts  1.67 us (2%)
    pallas_call x1, Pallas kernels, per_device(): pl.pallas_call(functools.partial(kernel, sizes), out_shape=jax.ShapeDtype...  78.7 us
    unnamed x1, local copies, waits for them, and re-layouts  1.67 us

profile of v2, /device:TPU:81, one launch (start us, length us, event | category | flops | bytes accessed | tf_op | source)
XLA Modules:
  0.0 80.4 jit_solution(5132723957599158810)
XLA Ops:
  0.0 78.7 %shard_map.55 = f32[512,128]{1,0:T(8,128)} custom-call(f32[512,128]{1,0:T(8,128)} %bitcast.6, f32[512,128]{1,0:T(8,128)} %bitcast.7, f32[1,64]{1,0:T(1,128)} %bitcast.9, s32[8,128]{1,0:T(8,128)} %bore_ref.1, s32[2,16]{1,0:T(2,128)} %bitcast.8), custom_call_target="tpu_custom_call" | custom-call | tf_op jit(solution)/shard_map/pallas_call | solution.py:499
  78.7 1.7 %copy.7 = f32[1,64,8,128]{3,2,1,0:T(8,128)} copy(f32[1,64,8,128]{3,2,1,0:T(8,128)} %bitcast.5) | data formatting | bytes 524288

commit v3 on v2

--- a/solution.py
+++ b/solution.py
@@ -47,7 +47,7 @@
     init_hbm, cap_hbm, prof_ref, bore_ref, plan_ref, out_ref,
     nat, src, xbuf, hbuf, bext, plans, rates, mom, pay, coef, sums_x, sums_y,
     load_sem, bore_send, bore_recv, plan_send, plan_recv, halo_send, halo_recv,
-    sum_send, sum_recv, shift_send, shift_recv,
+    sum_send, sum_recv, shift_send, shift_recv, part_send, part_recv,
     heat, inv, dinv, u0, ku, ca, cg, xs, v0s, v1s, v2s, *ts,
 ):
     slices, nx, ny = sizes
@@ -84,46 +84,21 @@
         @pl.when(tm >= s)
         def _():
             pl.semaphore_signal(barrier, inc=1, device_id={"tm": tm - s}, device_id_type=MESH)
-    greeted = nx - 1 + ny - 1
-    for a, b in around:
-        if a and b:
-            greeted = greeted + jnp.where(has(a, b), 1, 0)
-    for s in spans:
-        greeted = greeted + jnp.where(tm + s < slices, 1, 0)
-    pl.semaphore_wait(barrier, greeted)
 
     lane = lax.broadcasted_iota(jnp.int32, (8, 128), 1)
 
-    plans[0] = jnp.zeros((8, 128), jnp.int32)
-    plans[0, 0:STEPS, 0:LOOPS] = plan_ref[...]
-    bext[1, 8:16, :] = bore_ref[...]
-    for n, (a, b) in enumerate(around):
-        @pl.when(has(a, b))
-        def _():
-            pltpu.make_async_remote_copy(
-                src_ref=bore_ref, dst_ref=bext.at[1 - b, pl.ds(8 * (1 - a), 8), :],
-                send_sem=bore_send.at[n], recv_sem=bore_recv.at[n],
-                device_id={"gx": gx + a, "gy": gy + b}, device_id_type=MESH,
-            ).start()
-    for s in range(1, slots):
-        @pl.when(tm + 2 * s < slices)
-        def _():
-            pltpu.make_async_remote_copy(
-                src_ref=plans.at[0], dst_ref=plans.at[s],
-                send_sem=plan_send.at[s], recv_sem=plan_recv.at[s],
-                device_id={"tm": tm + 2 * s}, device_id_type=MESH,
-            ).start()
-
-    def halo_copy(e, at, n, a, b):
+    def halo_copy(e, at, n, a, b, q=None):
         rows = pl.ds(LOW, NYL) if b == 0 else pl.ds(LOW, 8) if b < 0 else pl.ds(HIGH - 8, 8)
+        lines, first = (HALF, 0) if q is None else (1, q)
         if a == 0:
             dst = hbuf.at[e, 1 if b < 0 else 0]
         else:
             at_rows = pl.ds(8, NYL) if b == 0 else pl.ds(8 + NYL, 8) if b < 0 else pl.ds(0, 8)
-            dst = xbuf.at[e, 1 if a < 0 else 0, :, at_rows, :]
+            dst = xbuf.at[e, 1 if a < 0 else 0, pl.ds(first, lines), at_rows, :]
         return pltpu.make_async_remote_copy(
-            src_ref=at.at[pl.ds(OWN, HALF), rows, :], dst_ref=dst,
-            send_sem=halo_send.at[e, n], recv_sem=halo_recv.at[e, n],
+            src_ref=at.at[pl.ds(OWN + first, lines), rows, :], dst_ref=dst,
+            send_sem=halo_send.at[e, n] if q is None else part_send.at[q, n],
+            recv_sem=halo_recv.at[e, n] if q is None else part_recv.at[q, n],
             device_id={"gx": gx + a, "gy": gy + b}, device_id_type=MESH,
         )
 
@@ -168,6 +143,33 @@
 
     load_cap.wait()
     to_wide(0, heat)
+    greeted = nx - 1 + ny - 1
+    for a, b in around:
+        if a and b:
+            greeted = greeted + jnp.where(has(a, b), 1, 0)
+    for s in spans:
+        greeted = greeted + jnp.where(tm + s < slices, 1, 0)
+    pl.semaphore_wait(barrier, greeted)
+    plans[0] = jnp.zeros((8, 128), jnp.int32)
+    plans[0, 0:STEPS, 0:LOOPS] = plan_ref[...]
+    bext[1, 8:16, :] = bore_ref[...]
+    for n, (a, b) in enumerate(around):
+        @pl.when(has(a, b))
+        def _():
+            pltpu.make_async_remote_copy(
+                src_ref=bore_ref, dst_ref=bext.at[1 - b, pl.ds(8 * (1 - a), 8), :],
+                send_sem=bore_send.at[n], recv_sem=bore_recv.at[n],
+                device_id={"gx": gx + a, "gy": gy + b}, device_id_type=MESH,
+            ).start()
+    for s in range(1, slots):
+        @pl.when(tm + 2 * s < slices)
+        def _():
+            pltpu.make_async_remote_copy(
+                src_ref=plans.at[0], dst_ref=plans.at[s],
+                send_sem=plan_send.at[s], recv_sem=plan_recv.at[s],
+                device_id={"tm": tm + 2 * s}, device_id_type=MESH,
+            ).start()
+
     halo_start(0, heat)
     load_init.wait()
     to_wide(1, u0)
@@ -269,6 +271,8 @@
         ku[1:WIDE, r:r + n, :] = 6.0 * mid - total
 
     zero = jnp.zeros((8, 128), f32)
+    early, late = list(range(slots - 1, slots // 2 - 1, -1)), list(range(slots // 2 - 1, -1, -1))
+    group_of = {s: g for g, group in enumerate((early, late)) for s in group}
 
     def krylov(n_step, s, first):
         x, v0, v1, v2 = xs.at[s], v0s.at[s], v1s.at[s], v2s.at[s]
@@ -297,28 +301,49 @@
             mid, total = beside(v2, OWN, r, n)
             sums[5] = add_own(sums[5], mid * total, OWN, r, n)
         for j, total in enumerate(sums):
-            mom[n_step, j, pl.ds(s, 1), :] = jnp.sum(total, axis=0, keepdims=True)
-
-    def total_over_tiles(n_step):
+            mom[n_step, group_of[s], j, s:s + 1, :] = jnp.sum(total, axis=0, keepdims=True)
+
+    stages = (("gx", nx, gx, sums_x), ("gy", ny, gy, sums_y))
+
+    def sum_copy(n_step, g, stage, d):
+        axis, count, me, buf = stages[stage]
+        return pltpu.make_async_remote_copy(
+            src_ref=pay.at[n_step, g, stage], dst_ref=buf.at[n_step, g, d],
+            send_sem=sum_send.at[n_step, g, stage, d], recv_sem=sum_recv.at[n_step, g, stage, d],
+            device_id={axis: lax.rem(me + d, count)}, device_id_type=MESH,
+        )
+
+    def sum_send_all(n_step, g, stage):
+        for d in range(1, stages[stage][1]):
+            sum_copy(n_step, g, stage, d).start()
+
+    def sum_collect(n_step, g, stage):
+        for d in range(1, stages[stage][1]):
+            sum_copy(n_step, g, stage, d).wait_recv()
+        total = pay[n_step, g, stage]
+        for d in range(1, stages[stage][1]):
+            total = total + stages[stage][3][n_step, g, d]
+        return total
+
+    def sum_start(n_step, g):
         packed = jnp.zeros((8, 128), f32)
         for j in range(6):
-            packed = jnp.where(lane == j, jnp.sum(mom[n_step, j], axis=1, keepdims=True), packed)
-        for stage, (axis, count, me, buf) in enumerate((("gx", nx, gx, sums_x), ("gy", ny, gy, sums_y))):
-            pay[n_step, stage] = packed
-            copies = []
-            for d in range(1, count):
-                copies.append(pltpu.make_async_remote_copy(
-                    src_ref=pay.at[n_step, stage], dst_ref=buf.at[n_step, d],
-                    send_sem=sum_send.at[n_step, stage, d], recv_sem=sum_recv.at[n_step, stage, d],
-                    device_id={axis: lax.rem(me + d, count)}, device_id_type=MESH,
-                ))
-                copies[-1].start()
-            for d, copy in enumerate(copies):
-                copy.wait_recv()
-                packed = packed + buf[n_step, d + 1]
-            for copy in copies:
-                copy.wait_send()
-        return [jnp.broadcast_to(packed[:, j:j + 1], (8, 128)) for j in range(6)]
+            packed = jnp.where(lane == j, jnp.sum(mom[n_step, g, j], axis=1, keepdims=True), packed)
+        pay[n_step, g, 0] = packed
+        sum_send_all(n_step, g, 0)
+
+    def sum_turn(n_step, g):
+        pay[n_step, g, 1] = sum_collect(n_step, g, 0)
+        sum_send_all(n_step, g, 1)
+
+    def sum_finish(n_step, g):
+        total = sum_collect(n_step, g, 1)
+        weights = cg_coefficients([jnp.broadcast_to(total[:, j:j + 1], (8, 128)) for j in range(6)])
+        for i in range(3):
+            coef[n_step, g, i] = weights[i]
+        for stage in range(2):
+            for d in range(1, stages[stage][1]):
+                sum_copy(n_step, g, stage, d).wait_send()
 
     def cg_coefficients(mu):
         def inner(p, q, m):
@@ -347,31 +372,48 @@
                 inner_now = inner_next
         return x
 
-    for n_step, first in ((0, 1), (1, 4)):
-        def each(s, _):
-            krylov(n_step, s, first)
-            return _
-
-        mom[n_step] = jnp.zeros((6, 8, 128), f32)
-        lax.fori_loop(0, slots, each, 0)
-        weights = cg_coefficients(total_over_tiles(n_step))
-        for i in range(3):
-            coef[n_step, i] = weights[i]
-
-        def update(s, _):
-            w = [coef[n_step, i, pl.ds(s, 1), :].reshape(1, 1, 128) for i in range(3)]
-            flag = jnp.where(tm - 2 * s == 0, f32(1.0), f32(0.0))
-            begin = 3 if n_step == 0 else OWN
-            for r, n in blocks(begin, n_step == 0):
-                here = (s, slice(begin, WIDE), slice(r, r + n))
-                value = w[0] * v0s[here] + w[1] * v1s[here] + w[2] * v2s[here]
-                if n_step == 0:
-                    xs[here] = value + flag * u0[begin:WIDE, r:r + n, :]
-                else:
-                    xs[here] = jnp.where(tm - 2 * s >= 0, value + xs[here], f32(0.0))
-            return _
-
-        lax.fori_loop(0, slots, update, 0)
+    def update(n_step, s):
+        w = [coef[n_step, group_of[s], i, s:s + 1, :].reshape(1, 1, 128) for i in range(3)]
+        flag = jnp.where(tm - 2 * s == 0, f32(1.0), f32(0.0))
+        begin = 3 if n_step == 0 else OWN
+        for r, n in blocks(begin, n_step == 0):
+            here = (s, slice(begin, WIDE), slice(r, r + n))
+            value = w[0] * v0s[here] + w[1] * v1s[here] + w[2] * v2s[here]
+            if n_step == 0:
+                xs[here] = value + flag * u0[begin:WIDE, r:r + n, :]
+            else:
+                xs[here] = jnp.where(tm - 2 * s >= 0, value + xs[here], f32(0.0))
+
+    def solve(n_step, group, between=None):
+        for i, s in enumerate(group):
+            if i == len(group) - 1 and between is not None:
+                between()
+            krylov(n_step, s, (1, 4)[n_step])
+
+    mom[...] = jnp.zeros(mom.shape, f32)
+    solve(0, early)
+    sum_start(0, 0)
+    if late:
+        solve(0, late, lambda: sum_turn(0, 0))
+        sum_start(0, 1)
+    else:
+        sum_turn(0, 0)
+    sum_finish(0, 0)
+    for s in early:
+        update(0, s)
+    solve(1, early, (lambda: sum_turn(0, 1)) if late else None)
+    sum_start(1, 0)
+    if late:
+        sum_finish(0, 1)
+        for s in late:
+            update(0, s)
+        solve(1, late, lambda: sum_turn(1, 0))
+        sum_start(1, 1)
+    else:
+        sum_turn(1, 0)
+    sum_finish(1, 0)
+    for s in early:
+        update(1, s)
 
     plan_rows = []
     span = slots // 2
@@ -390,35 +432,59 @@
             out = jnp.where(p == i, values[i], out)
         return out
 
-    shift = pltpu.make_async_remote_copy(
-        src_ref=xs.at[0, pl.ds(OWN, HALF), pl.ds(LOW, NYL), :],
-        dst_ref=xs.at[slots, pl.ds(OWN, HALF), pl.ds(LOW, NYL), :],
-        send_sem=shift_send.at[0], recv_sem=shift_recv.at[0],
-        device_id={"tm": lax.rem(tm + 1, slices)}, device_id_type=MESH,
-    )
+    def shift(q):
+        return pltpu.make_async_remote_copy(
+            src_ref=xs.at[0, pl.ds(OWN + q, 1), pl.ds(LOW, NYL), :],
+            dst_ref=xs.at[slots, pl.ds(OWN + q, 1), pl.ds(LOW, NYL), :],
+            send_sem=shift_send.at[q], recv_sem=shift_recv.at[q],
+            device_id={"tm": lax.rem(tm + 1, slices)}, device_id_type=MESH,
+        )
+
+    across = [(n, a) for n, (a, b) in enumerate(around) if b == 0]
 
     def pass_on():
+        state = xs.at[slots]
+
         @pl.when(tm < slices - 1)
         def _():
-            shift.start()
+            for q in range(HALF):
+                shift(q).start()
 
         @pl.when(tm == 0)
         def _():
             xs[slots, OWN:WIDE, LOW:HIGH, :] = jnp.zeros((HALF, NYL, 128), f32)
 
-        @pl.when(tm > 0)
-        def _():
-            shift.wait_recv()
-
-        halo_start(2 + last, xs.at[slots])
+        for q in range(HALF):
+            @pl.when(tm > 0)
+            def _():
+                shift(q).wait_recv()
+
+            for n, a in across:
+                @pl.when(has(a, 0))
+                def _():
+                    halo_copy(2 + last, state, n, a, 0, q).start()
+        for n, (a, b) in enumerate(around):
+            if b != 0:
+                @pl.when(has(a, b))
+                def _():
+                    halo_copy(2 + last, state, n, a, b).start()
 
         @pl.when(tm < slices - 1)
         def _():
-            shift.wait_send()
-
-    for s in order[:-1]:
-        if finished[s] < 0:
-            halo_start(2 + order.index(s), xs.at[s])
+            for q in range(HALF):
+                shift(q).wait_send()
+
+    waiting = [s for s in order[:-1] if finished[s] < 0]
+    if waiting:
+        halo_start(2 + order.index(waiting[0]), xs.at[waiting[0]])
+    if late:
+        sum_turn(1, 1)
+    for s in waiting[1:]:
+        halo_start(2 + order.index(s), xs.at[s])
+    if late:
+        sum_finish(1, 1)
+        for s in late:
+            update(1, s)
     if last == 0:
         pass_on()
 
@@ -434,7 +500,20 @@
             ca[:, r:r + n, :] = a
             cg[:, r:r + n, :] = 6.0 * a - 2.0
         ts[0][OWN:WIDE, LOW:HIGH, :] = xs[at, OWN:WIDE, LOW:HIGH, :]
-        halo_wait(2 + p, xs.at[at])
+        for n, (a, b) in enumerate(around):
+            if b != 0:
+                @pl.when(has(-a, -b))
+                def _():
+                    halo_copy(2 + p, xs.at[at], n, a, b).wait_recv()
+            else:
+                @pl.when(has(-a, -b) & (p < last))
+                def _():
+                    halo_copy(2 + p, xs.at[at], n, a, b).wait_recv()
+
+                @pl.when(has(-a, -b) & (p == last))
+                def _():
+                    for q in range(HALF):
+                        halo_copy(2 + p, xs.at[at], n, a, b, q).wait_recv()
         halo_build(2 + p, ts[0])
         for j in range(1, TERMS - 1):
             for r, n in blocks(j, True):
@@ -477,7 +556,11 @@
             halo_copy(0, heat, n, a, b).wait_send()
             halo_copy(1, u0, n, a, b).wait_send()
             for p, s in enumerate(order):
-                halo_copy(2 + p, xs.at[s], n, a, b).wait_send()
+                if p == last and b == 0:
+                    for q in range(HALF):
+                        halo_copy(2 + p, xs.at[s], n, a, b, q).wait_send()
+                else:
+                    halo_copy(2 + p, xs.at[s], n, a, b).wait_send()
     for s in range(1, slots):
         @pl.when(tm + 2 * s < slices)
         def _():
@@ -515,11 +598,11 @@
             pltpu.VMEM((3, 24, 128), jnp.int32),
             pltpu.VMEM((slots, 8, 128), jnp.int32),
             pltpu.VMEM((slots * STEPS * (NYL + 16), 128), f32),
-            pltpu.VMEM((STEPS, 6, 8, 128), f32),
-            pltpu.VMEM((STEPS, 2, 8, 128), f32),
-            pltpu.VMEM((STEPS, 3, 8, 128), f32),
-            pltpu.VMEM((STEPS, 8, 8, 128), f32),
-            pltpu.VMEM((STEPS, 8, 8, 128), f32),
+            pltpu.VMEM((STEPS, 2, 6, 8, 128), f32),
+            pltpu.VMEM((STEPS, 2, 2, 8, 128), f32),
+            pltpu.VMEM((STEPS, 2, 3, 8, 128), f32),
+            pltpu.VMEM((STEPS, 2, 8, 8, 128), f32),
+            pltpu.VMEM((STEPS, 2, 8, 8, 128), f32),
             dma((3,)),
             dma((8,)),
             dma((8,)),
@@ -527,10 +610,12 @@
             dma((slots,)),
             dma((exchanges, 8)),
             dma((exchanges, 8)),
-            dma((STEPS, 2, 8)),
-            dma((STEPS, 2, 8)),
-            dma((1,)),
-            dma((1,)),
+            dma((STEPS, 2, 2, 8)),
+            dma((STEPS, 2, 2, 8)),
+            dma((HALF,)),
+            dma((HALF,)),
+            dma((HALF, 8)),
+            dma((HALF, 8)),
         ] + [pltpu.VMEM(wide, f32)] * 7 + [pltpu.VMEM((slots + 1, *wide), f32)]
         + [pltpu.VMEM((slots, *wide), f32)] * 3 + [pltpu.VMEM(wide, f32)] * (TERMS - 1),
         compiler_params=pltpu.CompilerParams(

time: 80.6 us -> 78.2 us (0.970)
  the two profiles are of different devices: /device:TPU:81 before, /device:TPU:65 now
where the time goes in v3:
time: 78.2 us; the launch traced here: 78 us
  Pallas kernels  76.4 us (98%)
  local copies, waits for them, and re-layouts  1.67 us (2%)
    pallas_call x1, Pallas kernels, per_device(): pl.pallas_call(functools.partial(kernel, sizes), out_shape=jax.ShapeDtype...  76.4 us
    unnamed x1, local copies, waits for them, and re-layouts  1.67 us

profile of v3, /device:TPU:65, one launch (start us, length us, event | category | flops | bytes accessed | tf_op | source)
XLA Modules:
  0.0 78.0 jit_solution(16312989718414193127)
XLA Ops:
  0.0 76.4 %shard_map.55 = f32[512,128]{1,0:T(8,128)} custom-call(f32[512,128]{1,0:T(8,128)} %bitcast.6, f32[512,128]{1,0:T(8,128)} %bitcast.7, f32[1,64]{1,0:T(1,128)} %bitcast.9, s32[8,128]{1,0:T(8,128)} %bore_ref.1, s32[2,16]{1,0:T(2,128)} %bitcast.8), custom_call_target="tpu_custom_call" | custom-call | tf_op jit(solution)/shard_map/pallas_call | solution.py:582
  76.4 1.7 %copy.7 = f32[1,64,8,128]{3,2,1,0:T(8,128)} copy(f32[1,64,8,128]{3,2,1,0:T(8,128)} %bitcast.5) | data formatting | bytes 524288

commit v4 on v3

--- a/solution.py
+++ b/solution.py
@@ -24,6 +24,8 @@
 ROWS = NYL + 32
 LOW, HIGH = 16, 16 + NYL
 CHUNK = 16
+MID = LOW + NYL // 2
+PARTS = ((LOW, NYL // 2), (MID, 8), (MID + 8, NYL // 2 - 8))
 
 
 def cheb_coeffs(term_count):
@@ -88,19 +90,43 @@
     lane = lax.broadcasted_iota(jnp.int32, (8, 128), 1)
 
     def halo_copy(e, at, n, a, b, q=None):
-        rows = pl.ds(LOW, NYL) if b == 0 else pl.ds(LOW, 8) if b < 0 else pl.ds(HIGH - 8, 8)
-        lines, first = (HALF, 0) if q is None else (1, q)
+        first, size = (LOW, NYL) if q is None else PARTS[q]
+        rows = pl.ds(first, size) if b == 0 else pl.ds(LOW, 8) if b < 0 else pl.ds(HIGH - 8, 8)
         if a == 0:
             dst = hbuf.at[e, 1 if b < 0 else 0]
         else:
-            at_rows = pl.ds(8, NYL) if b == 0 else pl.ds(8 + NYL, 8) if b < 0 else pl.ds(0, 8)
-            dst = xbuf.at[e, 1 if a < 0 else 0, pl.ds(first, lines), at_rows, :]
+            at_rows = pl.ds(first - LOW + 8, size) if b == 0 else pl.ds(8 + NYL, 8) if b < 0 else pl.ds(0, 8)
+            dst = xbuf.at[e, 1 if a < 0 else 0, :, at_rows, :]
         return pltpu.make_async_remote_copy(
-            src_ref=at.at[pl.ds(OWN + first, lines), rows, :], dst_ref=dst,
-            send_sem=halo_send.at[e, n] if q is None else part_send.at[q, n],
-            recv_sem=halo_recv.at[e, n] if q is None else part_recv.at[q, n],
+            src_ref=at.at[pl.ds(OWN, HALF), rows, :], dst_ref=dst,
+            send_sem=halo_send.at[e, n] if q is None else part_send.at[e, q, n],
+            recv_sem=halo_recv.at[e, n] if q is None else part_recv.at[e, q, n],
             device_id={"gx": gx + a, "gy": gy + b}, device_id_type=MESH,
         )
+
+    def parts_start(e, at, parts, sides):
+        for n, (a, b) in enumerate(around):
+            if b in sides:
+                @pl.when(has(a, b))
+                def _():
+                    halo_copy(e, at, n, a, b).start()
+        for q in parts:
+            for n, (a, b) in enumerate(around):
+                if b == 0:
+                    @pl.when(has(a, b))
+                    def _():
+                        halo_copy(e, at, n, a, b, q).start()
+
+    def parts_wait(e, at, parts, side):
+        for n, (a, b) in enumerate(around):
+            if b == side or b == 0:
+                @pl.when(has(-a, -b))
+                def _():
+                    if b == 0:
+                        for q in parts:
+                            halo_copy(e, at, n, a, b, q).wait_recv()
+                    else:
+                        halo_copy(e, at, n, a, b).wait_recv()
 
     def halo_start(e, at):
         for n, (a, b) in enumerate(around):
@@ -118,9 +144,9 @@
 
     low_lanes = lax.broadcasted_iota(jnp.int32, (1, 8, 128), 2) < NZ
 
-    def halo_build(e, at):
-        for r, n in [(0, 8), (8, NYL), (8 + NYL, 8)]:
-            edge = down if r == 0 else up if r > 8 else True
+    def halo_build(e, at, segments=((0, 8), (8, NYL), (8 + NYL, 8))):
+        for r, n in segments:
+            edge = down if r == 0 else up if r == 8 + NYL else True
             for crossed in (False, True):
                 from_left = (~low_lanes if crossed else low_lanes) & left & edge
                 from_right = (low_lanes if crossed else ~low_lanes) & right & edge
@@ -132,8 +158,10 @@
                     if crossed:
                         value = pltpu.roll(value, NZ, 2)
                     at[m, LOW - 8 + r:LOW - 8 + r + n, :] = value.reshape(n, 128)
-        at[OWN:WIDE, LOW - 8:LOW, :] = jnp.where(down, hbuf[e, 0], f32(0.0))
-        at[OWN:WIDE, HIGH:HIGH + 8, :] = jnp.where(up, hbuf[e, 1], f32(0.0))
+        if (0, 8) in segments:
+            at[OWN:WIDE, LOW - 8:LOW, :] = jnp.where(down, hbuf[e, 0], f32(0.0))
+        if (8 + NYL, 8) in segments:
+            at[OWN:WIDE, HIGH:HIGH + 8, :] = jnp.where(up, hbuf[e, 1], f32(0.0))
 
     def to_wide(which, at):
         for q in range(HALF):
@@ -141,8 +169,6 @@
             low = nat[which, pl.ds(NXL - 1 - q, NZ, stride=NXL), :]
             at[OWN + q, LOW:HIGH, :] = jnp.concatenate([top, low], axis=0).T
 
-    load_cap.wait()
-    to_wide(0, heat)
     greeted = nx - 1 + ny - 1
     for a, b in around:
         if a and b:
@@ -170,6 +196,8 @@
                 device_id={"tm": tm + 2 * s}, device_id_type=MESH,
             ).start()
 
+    load_cap.wait()
+    to_wide(0, heat)
     halo_start(0, heat)
     load_init.wait()
     to_wide(1, u0)
@@ -204,30 +232,34 @@
 
     SPAN = NYL + 16
     loops = jnp.concatenate([bext[0], bext[1], bext[2]], axis=0)
-    for s in range(slots):
-        table = plans[s].astype(f32) - 3.5
-        for n in range(STEPS):
-            at_row = (s * STEPS + n) * SPAN
+    depth = jnp.concatenate([prof_ref[...], prof_ref[...]], axis=1)
+
+    def sources(n_step, first):
+        for s in range(slots):
+            table = plans[s].astype(f32) - 3.5
             rate = jnp.zeros((72, 128), f32)
             for v in range(LOOPS):
-                rate = jnp.where(loops == v, jnp.broadcast_to(table[n:n + 1, v:v + 1], (72, 128)), rate)
+                rate = jnp.where(loops == v, jnp.broadcast_to(table[n_step:n_step + 1, v:v + 1], (72, 128)), rate)
             turned = jnp.concatenate([rate, jnp.zeros((56, 128), f32)], axis=0).T
+            at_row = s * SPAN
             rates[at_row:at_row + 8, :] = pltpu.roll(turned[120:128, :], 24, 1)
             rates[at_row + 8:at_row + 8 + NYL, :] = turned
             rates[at_row + 8 + NYL:at_row + SPAN, :] = pltpu.roll(turned[0:8, :], 104, 1)
-    depth = jnp.concatenate([prof_ref[...], prof_ref[...]], axis=1)
-
-    def spread(m, _):
-        here = 32 + m - REACH
-        there = 32 + NXL - 1 - (m - REACH)
-        pick_row = lax.broadcasted_iota(jnp.int32, (128, 128), 0)
-        pick_lane = lax.broadcasted_iota(jnp.int32, (128, 128), 1)
-        pick = jnp.where(pick_row == jnp.where(pick_lane < NZ, here, there), f32(1.0), f32(0.0)).astype(jnp.bfloat16)
-        wide = jnp.dot(rates[...].astype(jnp.bfloat16), pick, preferred_element_type=f32)
-        src[m] = wide * depth
-        return _
-
-    lax.fori_loop(1, WIDE, spread, 0)
+        all_rates = rates[...].astype(jnp.bfloat16)
+
+        def spread(m, carry):
+            here = 32 + m - REACH
+            there = 32 + NXL - 1 - (m - REACH)
+            pick_row = lax.broadcasted_iota(jnp.int32, (128, 128), 0)
+            pick_lane = lax.broadcasted_iota(jnp.int32, (128, 128), 1)
+            pick = jnp.where(pick_row == jnp.where(pick_lane < NZ, here, there), f32(1.0), f32(0.0)).astype(jnp.bfloat16)
+            wide = jnp.dot(all_rates, pick, preferred_element_type=f32)
+            src[n_step, m] = wide * depth
+            return carry
+
+        lax.fori_loop(first, WIDE, spread, 0)
+
+    sources(0, 1)
 
     def rolled(value, by):
         return pltpu.roll(value, by, 2)
@@ -277,10 +309,10 @@
     def krylov(n_step, s, first):
         x, v0, v1, v2 = xs.at[s], v0s.at[s], v1s.at[s], v2s.at[s]
         flag = jnp.where(tm - 2 * s == 0, f32(1.0), f32(0.0))
-        base = s * (STEPS * SPAN) + n_step * SPAN
+        base = s * SPAN
         sums = [zero] * 6
         for r, n in blocks(first, True):
-            residual = src[first:WIDE, pl.ds(pl.multiple_of(base + (r - 8), 8), n), :]
+            residual = src[n_step, first:WIDE, base + (r - 8):base + (r - 8) + n, :]
             if n_step == 0:
                 residual = residual - flag * ku[first:WIDE, r:r + n, :]
             else:
@@ -384,33 +416,33 @@
             else:
                 xs[here] = jnp.where(tm - 2 * s >= 0, value + xs[here], f32(0.0))
 
-    def solve(n_step, group, between=None):
-        for i, s in enumerate(group):
-            if i == len(group) - 1 and between is not None:
-                between()
+    def solve(n_step, g, group):
+        for s in group:
             krylov(n_step, s, (1, 4)[n_step])
+        if group:
+            sum_start(n_step, g)
+
+    def turn_late(n_step):
+        if late:
+            sum_turn(n_step, 1)
 
     mom[...] = jnp.zeros(mom.shape, f32)
-    solve(0, early)
-    sum_start(0, 0)
-    if late:
-        solve(0, late, lambda: sum_turn(0, 0))
-        sum_start(0, 1)
-    else:
-        sum_turn(0, 0)
+    solve(0, 0, early)
+    solve(0, 1, late)
+    sum_turn(0, 0)
+    sources(1, 4)
+    turn_late(0)
     sum_finish(0, 0)
     for s in early:
         update(0, s)
-    solve(1, early, (lambda: sum_turn(0, 1)) if late else None)
-    sum_start(1, 0)
+    solve(1, 0, early)
     if late:
         sum_finish(0, 1)
-        for s in late:
-            update(0, s)
-        solve(1, late, lambda: sum_turn(1, 0))
-        sum_start(1, 1)
-    else:
-        sum_turn(1, 0)
+    for s in late:
+        update(0, s)
+    solve(1, 1, late)
+    sum_turn(1, 0)
+    turn_late(1)
     sum_finish(1, 0)
     for s in early:
         update(1, s)
@@ -432,60 +464,52 @@
             out = jnp.where(p == i, values[i], out)
         return out
 
-    def shift(q):
+    halves = ((LOW, MID), (MID, HIGH))
+
+    def shift(h):
+        rows = pl.ds(halves[h][0], NYL // 2)
         return pltpu.make_async_remote_copy(
-            src_ref=xs.at[0, pl.ds(OWN + q, 1), pl.ds(LOW, NYL), :],
-            dst_ref=xs.at[slots, pl.ds(OWN + q, 1), pl.ds(LOW, NYL), :],
-            send_sem=shift_send.at[q], recv_sem=shift_recv.at[q],
+            src_ref=xs.at[0, pl.ds(OWN, HALF), rows, :], dst_ref=xs.at[slots, pl.ds(OWN, HALF), rows, :],
+            send_sem=shift_send.at[h], recv_sem=shift_recv.at[h],
             device_id={"tm": lax.rem(tm + 1, slices)}, device_id_type=MESH,
         )
 
-    across = [(n, a) for n, (a, b) in enumerate(around) if b == 0]
+    def shift_start(h):
+        @pl.when(tm < slices - 1)
+        def _():
+            shift(h).start()
 
     def pass_on():
         state = xs.at[slots]
 
-        @pl.when(tm < slices - 1)
-        def _():
-            for q in range(HALF):
-                shift(q).start()
-
         @pl.when(tm == 0)
         def _():
             xs[slots, OWN:WIDE, LOW:HIGH, :] = jnp.zeros((HALF, NYL, 128), f32)
 
-        for q in range(HALF):
+        for h, parts, side in ((0, (0,), -1), (1, (1, 2), 1)):
             @pl.when(tm > 0)
             def _():
-                shift(q).wait_recv()
-
-            for n, a in across:
-                @pl.when(has(a, 0))
-                def _():
-                    halo_copy(2 + last, state, n, a, 0, q).start()
-        for n, (a, b) in enumerate(around):
-            if b != 0:
-                @pl.when(has(a, b))
-                def _():
-                    halo_copy(2 + last, state, n, a, b).start()
+                shift(h).wait_recv()
+
+            parts_start(2 + last, state, parts, (side,))
 
         @pl.when(tm < slices - 1)
         def _():
-            for q in range(HALF):
-                shift(q).wait_send()
+            for h in range(2):
+                shift(h).wait_send()
 
     waiting = [s for s in order[:-1] if finished[s] < 0]
     if waiting:
-        halo_start(2 + order.index(waiting[0]), xs.at[waiting[0]])
-    if late:
-        sum_turn(1, 1)
+        parts_start(2 + order.index(waiting[0]), xs.at[waiting[0]], (0, 1, 2), (-1, 1))
     for s in waiting[1:]:
-        halo_start(2 + order.index(s), xs.at[s])
+        parts_start(2 + order.index(s), xs.at[s], (0, 1, 2), (-1, 1))
     if late:
         sum_finish(1, 1)
         for s in late:
             update(1, s)
     if last == 0:
+        shift_start(0)
+        shift_start(1)
         pass_on()
 
     def combine(before, now, first, r, n):
@@ -500,36 +524,31 @@
             ca[:, r:r + n, :] = a
             cg[:, r:r + n, :] = 6.0 * a - 2.0
         ts[0][OWN:WIDE, LOW:HIGH, :] = xs[at, OWN:WIDE, LOW:HIGH, :]
-        for n, (a, b) in enumerate(around):
-            if b != 0:
-                @pl.when(has(-a, -b))
+        for h, parts, side, segments, (low, high) in (
+            (0, (0, 1), 1, ((0, 8), (8, NYL // 2 + 8)), (LOW - 8, MID + 8)),
+            (1, (2,), -1, ((16 + NYL // 2, NYL // 2 - 8), (8 + NYL, 8)), (MID, HIGH + 8)),
+        ):
+            parts_wait(2 + p, xs.at[at], parts, side)
+            halo_build(2 + p, ts[0], segments)
+            for j in range(1, TERMS - 1):
+                for r, n in chunks(low, high, CHUNK):
+                    mid, value, before = combine(ts[j - 2] if j > 1 else None, ts[j - 1], j, r, n)
+                    ts[j][j:WIDE, r:r + n, :] = 0.5 * value if j == 1 else value - before
+            for r, n in chunks(*halves[h], CHUNK):
+                mid, value, before = combine(ts[5], ts[6], OWN, r, n)
+                value = f32(cheb[7]) * (value - before) + f32(cheb[6]) * mid + f32(cheb[5]) * before
+                for j in range(5):
+                    value = value + f32(cheb[j]) * ts[j][OWN:WIDE, r:r + n, :]
+                xs[to, OWN:WIDE, r:r + n, :] = xs[to, OWN:WIDE, r:r + n, :] + value
+            if last > 0:
+                @pl.when(p == last - 1)
                 def _():
-                    halo_copy(2 + p, xs.at[at], n, a, b).wait_recv()
-            else:
-                @pl.when(has(-a, -b) & (p < last))
-                def _():
-                    halo_copy(2 + p, xs.at[at], n, a, b).wait_recv()
-
-                @pl.when(has(-a, -b) & (p == last))
-                def _():
-                    for q in range(HALF):
-                        halo_copy(2 + p, xs.at[at], n, a, b, q).wait_recv()
-        halo_build(2 + p, ts[0])
-        for j in range(1, TERMS - 1):
-            for r, n in blocks(j, True):
-                mid, value, before = combine(ts[j - 2] if j > 1 else None, ts[j - 1], j, r, n)
-                ts[j][j:WIDE, r:r + n, :] = 0.5 * value if j == 1 else value - before
-        for r, n in blocks(OWN, False):
-            mid, value, before = combine(ts[5], ts[6], OWN, r, n)
-            value = f32(cheb[7]) * (value - before) + f32(cheb[6]) * mid + f32(cheb[5]) * before
-            for j in range(5):
-                value = value + f32(cheb[j]) * ts[j][OWN:WIDE, r:r + n, :]
-            xs[to, OWN:WIDE, r:r + n, :] = xs[to, OWN:WIDE, r:r + n, :] + value
+                    shift_start(h)
         for s, p_done in finished.items():
             if p_done >= 0:
                 @pl.when(p == p_done)
                 def _():
-                    halo_start(2 + order.index(s), xs.at[s])
+                    parts_start(2 + order.index(s), xs.at[s], (0, 1, 2), (-1, 1))
         if last > 0:
             @pl.when(p == last - 1)
             def _():
@@ -556,8 +575,8 @@
             halo_copy(0, heat, n, a, b).wait_send()
             halo_copy(1, u0, n, a, b).wait_send()
             for p, s in enumerate(order):
-                if p == last and b == 0:
-                    for q in range(HALF):
+                if b == 0:
+                    for q in range(len(PARTS)):
                         halo_copy(2 + p, xs.at[s], n, a, b, q).wait_send()
                 else:
                     halo_copy(2 + p, xs.at[s], n, a, b).wait_send()
@@ -592,12 +611,12 @@
         out_specs=pl.BlockSpec(memory_space=pl.ANY),
         scratch_shapes=[
             pltpu.VMEM((2, NZ * NXL, NYL), f32),
-            pltpu.VMEM((WIDE, slots * STEPS * (NYL + 16), 128), f32),
+            pltpu.VMEM((STEPS, WIDE, slots * (NYL + 16), 128), f32),
             pltpu.VMEM((exchanges, 2, HALF, NYL + 16, 128), f32),
             pltpu.VMEM((exchanges, 2, HALF, 8, 128), f32),
             pltpu.VMEM((3, 24, 128), jnp.int32),
             pltpu.VMEM((slots, 8, 128), jnp.int32),
-            pltpu.VMEM((slots * STEPS * (NYL + 16), 128), f32),
+            pltpu.VMEM((slots * (NYL + 16), 128), f32),
             pltpu.VMEM((STEPS, 2, 6, 8, 128), f32),
             pltpu.VMEM((STEPS, 2, 2, 8, 128), f32),
             pltpu.VMEM((STEPS, 2, 3, 8, 128), f32),
@@ -612,10 +631,10 @@
             dma((exchanges, 8)),
             dma((STEPS, 2, 2, 8)),
             dma((STEPS, 2, 2, 8)),
-            dma((HALF,)),
-            dma((HALF,)),
-            dma((HALF, 8)),
-            dma((HALF, 8)),
+            dma((2,)),
+            dma((2,)),
+            dma((exchanges, len(PARTS), 8)),
+            dma((exchanges, len(PARTS), 8)),
         ] + [pltpu.VMEM(wide, f32)] * 7 + [pltpu.VMEM((slots + 1, *wide), f32)]
         + [pltpu.VMEM((slots, *wide), f32)] * 3 + [pltpu.VMEM(wide, f32)] * (TERMS - 1),
         compiler_params=pltpu.CompilerParams(

time: 78.2 us -> 73.6 us (0.941)
  the two profiles are of different devices: /device:TPU:65 before, /device:TPU:113 now
where the time goes in v4:
time: 73.6 us; the launch traced here: 73.4 us
  Pallas kernels  71.7 us (97%)
  local copies, waits for them, and re-layouts  1.67 us (2%)
    pallas_call x1, Pallas kernels, per_device(): pl.pallas_call(functools.partial(kernel, sizes), out_shape=jax.ShapeDtype...  71.7 us
    unnamed x1, local copies, waits for them, and re-layouts  1.67 us

profile of v4, /device:TPU:113, one launch (start us, length us, event | category | flops | bytes accessed | tf_op | source)
XLA Modules:
  0.0 73.4 jit_solution(11318894843449363460)
XLA Ops:
  0.0 71.7 %shard_map.55 = f32[512,128]{1,0:T(8,128)} custom-call(f32[512,128]{1,0:T(8,128)} %bitcast.6, f32[512,128]{1,0:T(8,128)} %bitcast.7, f32[1,64]{1,0:T(1,128)} %bitcast.9, s32[8,128]{1,0:T(8,128)} %bore_ref.1, s32[2,16]{1,0:T(2,128)} %bitcast.8), custom_call_target="tpu_custom_call" | custom-call | tf_op jit(solution)/shard_map/pallas_call | solution.py:601
  71.7 1.7 %copy.7 = f32[1,64,8,128]{3,2,1,0:T(8,128)} copy(f32[1,64,8,128]{3,2,1,0:T(8,128)} %bitcast.5) | data formatting | bytes 524288

commit v5 on v4

--- a/solution.py
+++ b/solution.py
@@ -129,7 +129,7 @@
                         halo_copy(e, at, n, a, b).wait_recv()
 
     def halo_start(e, at):
-        for n, (a, b) in enumerate(around):
+        for n, (a, b) in sorted(enumerate(around), key=lambda item: item[1][1] != 0):
             @pl.when(has(a, b))
             def _():
                 halo_copy(e, at, n, a, b).start()
@@ -373,9 +373,13 @@
         weights = cg_coefficients([jnp.broadcast_to(total[:, j:j + 1], (8, 128)) for j in range(6)])
         for i in range(3):
             coef[n_step, g, i] = weights[i]
-        for stage in range(2):
-            for d in range(1, stages[stage][1]):
-                sum_copy(n_step, g, stage, d).wait_send()
+
+    def sum_drain():
+        for n_step in range(STEPS):
+            for g in range(2 if late else 1):
+                for stage in range(2):
+                    for d in range(1, stages[stage][1]):
+                        sum_copy(n_step, g, stage, d).wait_send()
 
     def cg_coefficients(mu):
         def inner(p, q, m):
@@ -486,6 +490,7 @@
         def _():
             xs[slots, OWN:WIDE, LOW:HIGH, :] = jnp.zeros((HALF, NYL, 128), f32)
 
+        sum_drain()
         for h, parts, side in ((0, (0,), -1), (1, (1, 2), 1)):
             @pl.when(tm > 0)
             def _():
@@ -519,10 +524,15 @@
     def section(p, carry):
         at, to = pick(p, order), pick(p, [row[1] for row in plan_rows])
         factor = pick(p, [jnp.float32(2.0 * row[2] / (12.0 * slices)) for row in plan_rows])
-        for r, n in chunks(LOW - 8, HIGH + 8, CHUNK):
-            a = inv[:, r:r + n, :] * factor
-            ca[:, r:r + n, :] = a
-            cg[:, r:r + n, :] = 6.0 * a - 2.0
+        fresh = pick(p, [i == 0 or row[2] != plan_rows[i - 1][2] for i, row in enumerate(plan_rows)])
+
+        @pl.when(fresh)
+        def _():
+            for r, n in chunks(LOW - 8, HIGH + 8, CHUNK):
+                a = inv[:, r:r + n, :] * factor
+                ca[:, r:r + n, :] = a
+                cg[:, r:r + n, :] = 6.0 * a - 2.0
+
         ts[0][OWN:WIDE, LOW:HIGH, :] = xs[at, OWN:WIDE, LOW:HIGH, :]
         for h, parts, side, segments, (low, high) in (
             (0, (0, 1), 1, ((0, 8), (8, NYL // 2 + 8)), (LOW - 8, MID + 8)),
@@ -540,15 +550,15 @@
                 for j in range(5):
                     value = value + f32(cheb[j]) * ts[j][OWN:WIDE, r:r + n, :]
                 xs[to, OWN:WIDE, r:r + n, :] = xs[to, OWN:WIDE, r:r + n, :] + value
+            for s, p_done in finished.items():
+                if p_done >= 0:
+                    @pl.when(p == p_done)
+                    def _():
+                        parts_start(2 + order.index(s), xs.at[s], ((0,), (1, 2))[h], ((-1,), (1,))[h])
             if last > 0:
                 @pl.when(p == last - 1)
                 def _():
                     shift_start(h)
-        for s, p_done in finished.items():
-            if p_done >= 0:
-                @pl.when(p == p_done)
-                def _():
-                    parts_start(2 + order.index(s), xs.at[s], (0, 1, 2), (-1, 1))
         if last > 0:
             @pl.when(p == last - 1)
             def _():

time: 73.6 us -> 73.4 us (level)
  no operation moved by 1% of the time
where the time goes in v5:
time: 73.4 us; the launch traced here: 73.2 us
  Pallas kernels  71.6 us (98%)
  local copies, waits for them, and re-layouts  1.67 us (2%)
    pallas_call x1, Pallas kernels, per_device(): pl.pallas_call(functools.partial(kernel, sizes), out_shape=jax.ShapeDtype...  71.6 us
    unnamed x1, local copies, waits for them, and re-layouts  1.67 us

profile of v5, /device:TPU:113, one launch (start us, length us, event | category | flops | bytes accessed | tf_op | source)
XLA Modules:
  0.0 73.2 jit_solution(9150403639726205328)
XLA Ops:
  0.0 71.6 %shard_map.55 = f32[512,128]{1,0:T(8,128)} custom-call(f32[512,128]{1,0:T(8,128)} %bitcast.6, f32[512,128]{1,0:T(8,128)} %bitcast.7, f32[1,64]{1,0:T(1,128)} %bitcast.9, s32[8,128]{1,0:T(8,128)} %bore_ref.1, s32[2,16]{1,0:T(2,128)} %bitcast.8), custom_call_target="tpu_custom_call" | custom-call | tf_op jit(solution)/shard_map/pallas_call | solution.py:611
  71.6 1.7 %copy.7 = f32[1,64,8,128]{3,2,1,0:T(8,128)} copy(f32[1,64,8,128]{3,2,1,0:T(8,128)} %bitcast.5) | data formatting | bytes 524288
